TPU v7x, 128 devices: a whole 4x4x4 slice. The times are simulated.
128 devices in a mesh: row: 16 (over x_hi, y, core), col: 8 (over z, x_lo).
Axes of the slice: x: 4 (x_hi: 2, x_lo: 2; x = x_hi * 2 + x_lo), y: 4, z: 4, core: 2. Of those that a mesh axis runs over, the one named last changes fastest.
Arguments:
- hidden_states: bfloat16 [8192, 5120], P(None, 'row'), may hold values from -30 to 30
- lengths: int32 [32], replicated, may hold values from 64 to 256, as said below
- layer_norm_gain: float32 [5120], replicated, may hold values from 0.5 to 1.5
- layer_norm_bias: float32 [5120], replicated, may hold values from -3 to 3
- weights: float32 [4, 5120, 5120], P(None, ('row', 'col')), may hold values from -0.125 to 0.125
- adapter_down_factors: float32 [4, 64, 5120], replicated, may hold values from -0.1 to 0.1
- adapter_up_factors: float32 [4, 5120, 64], P(None, ('row', 'col')), may hold values from -2 to 2
Outputs:
- mixed: bfloat16 [8192, 5120], P('col', 'row')
Inputs may be any that keep to these rules, and one draw needn't show every extreme that they name: `lengths`: every protein has at least 64 residues and at least one has exactly 256.
All inputs are finite; a program needn't handle non-finite values.
Results may differ from a plain program's by a relative error of at most 0.02.
Values may be sent and summed in bfloat16 or wider, within the bound.
A program may use at most 192 MiB of HBM per device.

v0:
```python
import jax
import jax.numpy as jnp
from jax import lax
from jax.sharding import PartitionSpec as P

D = 5120
HEAD = 128
LEN = 256


adapter_scale = 2.0
ln_eps = 1e-05


def rotary_tables(length, head_dim):
    half_dim = head_dim // 2
    frequency = 10000.0 ** (-(2.0 * jnp.arange(half_dim, dtype=jnp.float32)) / head_dim)
    angles = jnp.arange(length, dtype=jnp.float32)[:, None] * frequency[None, :]
    angles = jnp.concatenate([angles, angles], axis=1)
    return (jnp.cos(angles), jnp.sin(angles))


def rotate(values, cosine_table, sine_table):
    half_dim = values.shape[-1] // 2
    turned = jnp.concatenate([-values[..., half_dim:], values[..., :half_dim]], axis=-1)
    return values * cosine_table[:, None, :] + turned * sine_table[:, None, :]


def normalize(embedded, first_sum, second_sum, gain_part, bias_part):
    average = first_sum[:, None] / D
    variance = second_sum[:, None] / D - average * average
    return ((embedded - average) * lax.rsqrt(variance + ln_eps) * gain_part + bias_part).astype(
        jnp.bfloat16
    )


def slot_valid(first_slot, slot_count, lengths):
    positions = first_slot + jnp.arange(slot_count, dtype=jnp.int32)
    protein = positions // LEN
    matches = protein[:, None] == jnp.arange(lengths.shape[0], dtype=jnp.int32)[None, :]
    length_of = jnp.sum(jnp.where(matches, lengths[None, :], 0), axis=1)
    return positions % LEN < length_of


def masked_rows(state_rows, is_valid):
    return state_rows.astype(jnp.float32) * is_valid[:, None].astype(jnp.float32)


def contract_last(left_rows, right_rows):
    return lax.dot_general(
        left_rows, right_rows, (((1,), (1,)), ((), ())), preferred_element_type=jnp.float32
    )


def per_device(
    hidden_states,
    lengths,
    layer_norm_gain,
    layer_norm_bias,
    weights,
    adapter_down_factors,
    adapter_up_factors,
):
    row_count = lax.axis_size("row")
    col_count = lax.axis_size("col")
    row_idx = lax.axis_index("row")
    col_idx = lax.axis_index("col")
    merged_weights = (
        weights
        + adapter_scale
        * jnp.einsum(
            "dvc,dcw->dvw",
            adapter_up_factors,
            adapter_down_factors,
            precision=lax.Precision.HIGHEST,
        )
    ).astype(jnp.bfloat16)
    shard_rows = merged_weights.shape[1]
    full_width = merged_weights.shape[2]
    in_part = full_width // row_count
    out_part = full_width // col_count
    group_size = row_count // col_count
    qkv_rows = lax.all_to_all(
        lax.all_to_all(merged_weights[:3], "row", split_axis=2, concat_axis=1, tiled=True),
        "col",
        split_axis=1,
        concat_axis=1,
        tiled=True,
    )
    qkv_block = qkv_rows.reshape(3, col_count, group_size, shard_rows, in_part)
    qkv_block = qkv_block.transpose(0, 2, 1, 3, 4).reshape(3 * out_part, in_part)
    out_block = lax.all_to_all(merged_weights[3], "col", split_axis=1, concat_axis=0, tiled=True)
    tokens = hidden_states.shape[0]
    local_rows = tokens // row_count
    first_token = row_idx * local_rows
    local_states = lax.all_to_all(hidden_states, "row", split_axis=0, concat_axis=1, tiled=True)
    embedded = masked_rows(local_states, slot_valid(first_token, local_rows, lengths))
    normed = normalize(
        embedded,
        jnp.sum(embedded, axis=1),
        jnp.sum(embedded * embedded, axis=1),
        layer_norm_gain,
        layer_norm_bias,
    )
    qkv = contract_last(normed, lax.all_gather(qkv_block, "row", axis=1, tiled=True))
    heads_dev = out_part // HEAD
    proteins_dev = local_rows // LEN
    cosine_table, sine_table = rotary_tables(LEN, HEAD)
    queries = rotate(
        qkv[:, :out_part].reshape(proteins_dev, LEN, heads_dev, HEAD), cosine_table, sine_table
    ).astype(jnp.bfloat16)
    key_rows = rotate(
        qkv[:, out_part : 2 * out_part].reshape(proteins_dev, LEN, heads_dev, HEAD),
        cosine_table,
        sine_table,
    ).astype(jnp.bfloat16)
    value_rows = (
        qkv[:, 2 * out_part :].reshape(proteins_dev, LEN, heads_dev, HEAD).astype(jnp.bfloat16)
    )
    local_lengths = lax.dynamic_slice_in_dim(lengths, row_idx * proteins_dev, proteins_dev, 0)
    scores = jnp.einsum(
        "pqhd,pkhd->phqk", queries, key_rows, preferred_element_type=jnp.float32
    ) * HEAD ** (-0.5)
    key_valid = jnp.arange(LEN, dtype=jnp.int32)[None, :] < local_lengths[:, None]
    scores = jnp.where(key_valid[:, None, None, :], scores, -jnp.inf)
    row_max = jnp.max(scores, axis=3, keepdims=True)
    exponent = jnp.exp(scores - row_max)
    soft_weights = (exponent / jnp.sum(exponent, axis=3, keepdims=True)).astype(jnp.bfloat16)
    attention = jnp.einsum(
        "phqk,pkhd->pqhd", soft_weights, value_rows, preferred_element_type=jnp.float32
    )
    attention = attention.astype(jnp.bfloat16).reshape(local_rows, out_part)
    all_heads = lax.all_gather(attention, "row", axis=0, tiled=True)
    out_rows = tokens // col_count
    projected = lax.psum_scatter(
        contract_last(all_heads, out_block).astype(jnp.bfloat16),
        "col",
        scatter_dimension=0,
        tiled=True,
    ).astype(jnp.float32)
    first_out = col_idx * out_rows
    out_states = lax.dynamic_slice_in_dim(hidden_states, first_out, out_rows, 0)
    residual = masked_rows(out_states, slot_valid(first_out, out_rows, lengths))
    return (residual + projected).astype(jnp.bfloat16)


def solution(mesh):
    in_specs = (
        P(None, "row"),
        P(),
        P(),
        P(),
        P(None, ("row", "col"), None),
        P(),
        P(None, ("row", "col"), None),
    )
    out_specs = P("col", "row")
    return jax.shard_map(
        per_device, mesh=mesh, in_specs=in_specs, out_specs=out_specs, check_vma=False
    )
```

profile of v0, /device:TPU:1, one launch (start us, length us, event | category | flops | bytes accessed | tf_op | source)
XLA Modules:
  0.0 526.2 jit_solution(13985002247015834927)
XLA Ops:
  7.4 6.8 %fusion.7 = bf16[4,40,5120]{2,1,0:T(8,128)(2,1)S(1)} fusion(f32[4,40,5120]{2,1,0:T(8,128)} %param.11, f32[4,40,64]{2,1,0:T(8,128)S(1)} %copy-done, f32[4,64,5120]{2,1,0:T(8,128)} %param.12), kind=kOutput, calls=%fused_computation.12 | convolution fusion | flops 631603200 | bytes 10199040 | tf_op jit(solution)/shard_map/dvc,dcw->dvw/dot_general | solution.py:71
  14.2 1.1 copy-done.2
  15.5 5.1 copy.55
  20.5 8.3 %reshape.203 = bf16[16,2,19200]{2,1,0:T(2,128)(2,1)S(1)} reshape(bf16[5120,3,40]{2,1,0:T(4,128)(2,1)} %bitcast.52) | data formatting | bytes 2457600
  28.8 27.5 %all_to_all.55 = bf16[16,2,19200]{2,1,0:T(2,128)(2,1)S(1)} all-to-all(bf16[16,2,19200]{2,1,0:T(2,128)(2,1)S(1)} %reshape.203), channel_id=1, replica_groups=mesh['row'=16,'col'=8] {'row'}, dimensions={0} | all-to-all | bytes 2457600 | tf_op jit(solution)/shard_map/all_to_all | solution.py:84
  56.4 7.5 %reshape.204 = bf16[5120,3,40]{2,1,0:T(4,128)(2,1)} reshape(bf16[16,2,19200]{2,1,0:T(2,128)(2,1)S(1)} %all_to_all.55) | data formatting | bytes 2457600
  63.9 6.0 %copy.56 = bf16[3,40,16,320]{3,1,2,0:T(8,128)(2,1)S(1)} copy(bf16[3,40,16,320]{1,0,3,2:T(4,128)(2,1)} %bitcast.53) | data formatting | bytes 2457600 | tf_op jit(solution)/shard_map/all_to_all | solution.py:84
  69.9 1.3 copy.57
  71.2 29.6 %all_to_all.56 = bf16[3,640,320]{2,0,1:T(4,128)(2,1)S(1)} all-to-all(bf16[3,640,320]{2,0,1:T(4,128)(2,1)S(1)} %copy.57), channel_id=1, replica_groups=mesh['row'=16,'col'=8] {'col'}, dimensions={1} | all-to-all | bytes 2457600 | tf_op jit(solution)/shard_map/all_to_all | solution.py:83
  101.0 2.0 copy.59
  103.1 5.3 %copy.98 = bf16[40,16,8,512]{3,2,0,1:T(8,128)(2,1)} copy(bf16[40,16,8,512]{3,2,1,0:T(8,128)(2,1)} %bitcast.55) | data formatting | bytes 10485760 | tf_op jit(solution)/shard_map/all_to_all | solution.py:96
  108.4 6.5 %all-to-all-start = ((bf16[16,512,320]{1,2,0:T(8,128)(2,1)}), bf16[16,512,320]{1,2,0:T(8,128)(2,1)}, u32[]{:S(2)}, u32[]{:S(2)}) async-start(bf16[16,512,320]{1,2,0:T(8,128)(2,1)} %bitcast.51), calls=%async_computation | async-start | bytes 10485760 | tf_op jit(solution)/shard_map/all_to_all | solution.py:96
  115.2 1.1 fusion.30
  116.5 77.2 %all-to-all-done = bf16[16,512,320]{1,2,0:T(8,128)(2,1)} async-done(((bf16[16,512,320]{1,2,0:T(8,128)(2,1)}), bf16[16,512,320]{1,2,0:T(8,128)(2,1)}, u32[]{:S(2)}, u32[]{:S(2)}) %all-to-all-start) | async-done | bytes 5242912 | tf_op jit(solution)/shard_map/all_to_all | solution.py:96
  193.6 4.3 multiply_reduce_fusion.1
  197.9 7.2 %fusion.5 = bf16[512,5120]{0,1:T(8,128)(2,1)} fusion(bf16[16,512,320]{1,2,0:T(8,128)(2,1)} %all-to-all-done, f32[5120]{0:T(1024)S(1)} %copy-done.5, f32[5120]{0:T(1024)S(1)} %copy-done.6, f32[512]{0:T(512)S(1)} %get-tuple-element.18, f32[512]{0:T(512)S(1)} %get-tuple-element.17, f32[512]{0:T(512)S(1)} %fusion.41), kind=kLoop, calls=%fused_computation.7 | loop fusion | flops 18350080 | bytes 10532864 | tf_op jit(solution)/shard_map/convert_element_type | solution.py:32
  205.1 72.3 %all-gather.3.cloned.1.call-done = bf16[1920,5120]{0,1:T(8,128)(2,1)} async-done(((bf16[1920,320]{0,1:T(8,128)(2,1)}), bf16[1920,5120]{0,1:T(8,128)(2,1)}) %all-gather.3.cloned.1.call-update) | async-done | bytes 19660816 | tf_op jit(solution)/shard_map/all_gather | solution.py:105
  277.3 16.3 %fusion.55 = f32[512,1920]{1,0:T(8,128)S(1)} fusion(bf16[512,5120]{0,1:T(8,128)(2,1)} %fusion.5, bf16[1920,5120]{0,1:T(8,128)(2,1)} %all-gather.3.cloned.1.call-done), kind=kOutput, calls=%fused_computation.79 | convolution fusion | flops 10066329600 | bytes 28835840 | tf_op jit(solution)/shard_map/dot_general | solution.py:50
  293.9 1.5 copy.62
  295.4 2.1 reshape.199
  297.5 1.5 copy.61
  299.0 2.1 reshape.198
  301.1 1.7 reshape.202
  302.8 1.2 slice_negate_fusion
  304.0 2.6 fusion.10
  306.6 3.7 fusion.50
  310.3 2.2 fusion.16
  314.3 12.5 %all_to_all.57 = bf16[40,8,640]{2,0,1:T(8,128)(2,1)S(1)} all-to-all(bf16[40,8,640]{2,0,1:T(8,128)(2,1)S(1)} %copy.68), channel_id=1, replica_groups=mesh['row'=16,'col'=8] {'col'}, dimensions={1} | all-to-all | bytes 819200 | tf_op jit(solution)/shard_map/all_to_all | solution.py:92
  326.8 72.6 %all-gather.5.cloned.1.call-done = bf16[8192,640]{0,1:T(8,128)(2,1)} async-done(((bf16[512,640]{0,1:T(8,128)(2,1)}), bf16[8192,640]{0,1:T(8,128)(2,1)}) %all-gather.5.cloned.1.call-update) | async-done | bytes 10485776 | tf_op jit(solution)/shard_map/all_gather | solution.py:133
  399.4 10.0 %convolution_convert_fusion = bf16[8192,320]{0,1:T(8,128)(2,1)} fusion(bf16[320,640]{1,0:T(8,128)(2,1)S(1)} %bitcast.62, bf16[8192,640]{0,1:T(8,128)(2,1)} %all-gather.5.cloned.1.call-done), kind=kOutput, calls=%fused_computation.1 | convolution fusion | flops 3358064640 | bytes 16138240 | tf_op jit(solution)/shard_map/dot_general | solution.py:50
  409.6 107.7 %reduce-scatter.2.cloned.1.call-done = bf16[1024,320]{0,1:T(8,128)(2,1)} async-done(((bf16[8192,320]{0,1:T(8,128)(2,1)}), bf16[1024,320]{0,1:T(8,128)(2,1)}) %reduce-scatter.2.cloned.1.call-update) | async-done | bytes 655376 | tf_op jit(solution)/shard_map/reduce_scatter | solution.py:135
  517.3 2.4 add_convert_fusion
  (42 shorter events, 3.8 us)
Async XLA Ops:
  6.5 0.9 copy-start
  6.5 270.8 %all-gather.3.cloned.1.call-start = ((), (), s32[]{:S(2)}) async-start(), calls=%async_computation.5 | async-start | bytes 20889600 | tf_op jit(solution)/shard_map/all_gather | solution.py:105
  14.2 1.2 copy-start.2
  108.4 6.5 %copy-start.7 = (s32[32]{0:T(128)S(1)}, s32[32]{0:T(128)}, u32[]{:S(2)}) copy-start(s32[32]{0:T(128)} %param.8) | copy-start | bytes 388
  108.4 85.2 %all-to-all-start = ((bf16[16,512,320]{1,2,0:T(8,128)(2,1)}), bf16[16,512,320]{1,2,0:T(8,128)(2,1)}, u32[]{:S(2)}, u32[]{:S(2)}) async-start(bf16[16,512,320]{1,2,0:T(8,128)(2,1)} %bitcast.51), calls=%async_computation | async-start | bytes 10485760 | tf_op jit(solution)/shard_map/all_to_all | solution.py:96
  114.9 284.5 %all-gather.5.cloned.1.call-start = ((), (), s32[]{:S(2)}) async-start(), calls=%async_computation.6 | async-start | bytes 11141120 | tf_op jit(solution)/shard_map/all_gather | solution.py:133
  116.4 81.5 %copy-start.5 = (f32[5120]{0:T(1024)S(1)}, f32[5120]{0:T(1024)}, u32[]{:S(2)}) copy-start(f32[5120]{0:T(1024)} %param.10) | copy-start | bytes 61444
  116.5 81.5 %copy-start.6 = (f32[5120]{0:T(1024)S(1)}, f32[5120]{0:T(1024)}, u32[]{:S(2)}) copy-start(f32[5120]{0:T(1024)} %param.9) | copy-start | bytes 61444
  302.8 1.2 copy-start.4
  306.6 3.7 copy-start.3
  312.5 1.7 slice-start
  314.1 203.2 %reduce-scatter.2.cloned.1.call-start = ((), (), s32[]{:S(2)}) async-start(), calls=%async_computation.7 | async-start | bytes 5898240 | tf_op jit(solution)/shard_map/reduce_scatter | solution.py:135
  409.4 110.3 %copy-start.1 = (f32[4,40,64]{2,1,0:T(8,128)S(1)}, f32[4,40,64]{2,1,0:T(8,128)}, u32[]{:S(2)}) copy-start(f32[4,40,64]{2,1,0:T(8,128)} %param.13) | copy-start | bytes 122884
Sparse Core Ops, SparseCore 0:
  103.2 174.0 all-gather.2
  314.2 85.1 all-gather.4
  409.6 107.7 reduce-scatter.1
where the time goes:
time: 527 us; the launch traced here: 526 us
  waiting for transfers between devices  330 us (63%)
  blocking collectives  69.7 us (13%)
  local copies, waits for them, and re-layouts  48.7 us (9%)
  matrix products  39 us (7%)
  other arithmetic  19.1 us (4%)
  between operations  13.3 us (3%)
  starting transfers between devices  6.57 us (1%)
    reduce_scatter x1, waiting for transfers between devices, per_device(): lax.psum_scatter(contract_last(all_heads, out_block).astype(jnp.bfloat16)...  108 us
    all_to_all x1, waiting for transfers between devices, per_device(): lax.all_to_all(hidden_states, 'row', split_axis=0, concat_axis=1, tiled=T...  77.2 us
    all_gather x1, waiting for transfers between devices, per_device(): all_heads = lax.all_gather(attention, 'row', axis=0, tiled=True)  72.6 us
    all_gather x1, waiting for transfers between devices, per_device(): lax.all_gather(qkv_block, 'row', axis=1, tiled=True)  72.3 us
    all_to_all x1, blocking collectives, per_device(): lax.all_to_all(lax.all_to_all(merged_weights[:3], 'row', split_axis=2, co...  29.6 us
    all_to_all x1, blocking collectives, per_device(): lax.all_to_all(merged_weights[:3], 'row', split_axis=2, concat_axis=1, ti...  27.5 us
    dot_general x2, matrix products, contract_last(): lax.dot_general(left_rows, right_rows, (((1,), (1,)), ((), ())), preferre...  26.3 us
    unnamed x20, local copies, waits for them, and re-layouts  18.8 us
  transfers between devices with their start and end apart: 4, of which 4 were waited for; matrix products, arithmetic and copies ran while one was open for 3% of the time, Pallas kernels for 0%

commit v1 on v0

v1 whole, which is shorter than its diff:
```python
import jax
import jax.numpy as jnp
from jax import lax
from jax.sharding import PartitionSpec as P

D = 5120
HEAD = 128
HALF = 64
LEN = 256

adapter_scale = 2.0
ln_eps = 1e-05


def rotary_tables(length, head_dim):
    half_dim = head_dim // 2
    frequency = 10000.0 ** (-(2.0 * jnp.arange(half_dim, dtype=jnp.float32)) / head_dim)
    angles = jnp.arange(length, dtype=jnp.float32)[:, None] * frequency[None, :]
    angles = jnp.concatenate([angles, angles], axis=1)
    return (jnp.cos(angles), jnp.sin(angles))


def rotate(values, cosine_table, sine_table):
    half_dim = values.shape[-1] // 2
    turned = jnp.concatenate([-values[..., half_dim:], values[..., :half_dim]], axis=-1)
    return values * cosine_table[:, None, :] + turned * sine_table[:, None, :]


def contract_last(left_rows, right_rows):
    return lax.dot_general(
        left_rows, right_rows, (((1,), (1,)), ((), ())), preferred_element_type=jnp.float32
    )


def attend(qkv, lengths, cosine_table, sine_table):
    queries = rotate(qkv[0], cosine_table, sine_table).astype(jnp.bfloat16)
    key_rows = rotate(qkv[1], cosine_table, sine_table).astype(jnp.bfloat16)
    value_rows = qkv[2].astype(jnp.bfloat16)
    scores = jnp.einsum(
        "pqhd,pkhd->phqk", queries, key_rows, preferred_element_type=jnp.float32
    ) * HEAD ** (-0.5)
    key_valid = jnp.arange(LEN, dtype=jnp.int32)[None, :] < lengths[:, None]
    scores = jnp.where(key_valid[:, None, None, :], scores, -jnp.inf)
    row_max = jnp.max(scores, axis=3, keepdims=True)
    exponent = jnp.exp(scores - row_max)
    soft = (exponent / jnp.sum(exponent, axis=3, keepdims=True)).astype(jnp.bfloat16)
    out = jnp.einsum("phqk,pkhd->pqhd", soft, value_rows, preferred_element_type=jnp.float32)
    out = out.astype(jnp.bfloat16)
    return out.reshape(out.shape[0] * LEN, -1)


def per_device(
    hidden_states,
    lengths,
    layer_norm_gain,
    layer_norm_bias,
    weights,
    adapter_down_factors,
    adapter_up_factors,
):
    col_count = lax.axis_size("col")
    row_count = lax.axis_size("row")
    row_idx = lax.axis_index("row")
    col_idx = lax.axis_index("col")
    core = row_idx % 2
    tokens = hidden_states.shape[0] // col_count
    proteins = tokens // LEN
    first = col_idx * tokens
    own = lax.dynamic_slice_in_dim(hidden_states, first, tokens, 0)
    states = lax.all_gather(own, "row", axis=1, tiled=True)
    merged = (
        weights
        + adapter_scale
        * jnp.einsum(
            "dvc,dcw->dvw",
            adapter_up_factors,
            adapter_down_factors,
            precision=lax.Precision.HIGHEST,
        )
    ).astype(jnp.bfloat16)
    local_lengths = lax.dynamic_slice_in_dim(lengths, col_idx * proteins, proteins, 0)
    valid = (jnp.arange(LEN, dtype=jnp.int32)[None, :] < local_lengths[:, None]).reshape(tokens)
    mask = valid[:, None].astype(jnp.float32)
    block = lax.all_gather(merged[:3], "col", axis=1, tiled=True)
    out_block = lax.all_gather(merged[3], "col", axis=0, tiled=True)
    part = block.shape[1]

    embedded = states.astype(jnp.float32) * mask
    average = jnp.sum(embedded, axis=1)[:, None] / D
    variance = jnp.sum(embedded * embedded, axis=1)[:, None] / D - average * average
    normed = (
        (embedded - average) * lax.rsqrt(variance + ln_eps) * layer_norm_gain + layer_norm_bias
    ).astype(jnp.bfloat16)
    qkv = contract_last(normed, block.reshape(3 * part, D)).reshape(tokens, 3, part)
    whole = part // HEAD * HEAD
    mine = lax.dynamic_slice_in_dim(qkv, core * HALF, whole, 2)
    half = lax.dynamic_slice_in_dim(qkv, (1 - core) * whole, HALF, 2)
    half_tokens = tokens // 2
    keep = lax.dynamic_slice_in_dim(half, core * half_tokens, half_tokens, 0)
    send = lax.dynamic_slice_in_dim(half, (1 - core) * half_tokens, half_tokens, 0)
    got = lax.ppermute(send, "row", [(i, i ^ 1) for i in range(row_count)])
    split = jnp.where(
        core == 0,
        jnp.concatenate([keep, got], axis=2),
        jnp.concatenate([got, keep], axis=2),
    )
    cosine_table, sine_table = rotary_tables(LEN, HEAD)
    mine = mine.transpose(1, 0, 2).reshape(3, proteins, LEN, whole // HEAD, HEAD)
    split = split.transpose(1, 0, 2).reshape(3, proteins // 2, LEN, 1, HEAD)
    split_lengths = lax.dynamic_slice_in_dim(local_lengths, core * (proteins // 2), proteins // 2, 0)
    attn_a = attend(mine, local_lengths, cosine_table, sine_table)
    attn_b = attend(split, split_lengths, cosine_table, sine_table)
    both = jnp.concatenate([attn_a, attn_b.reshape(tokens, HALF)], axis=1)
    got = lax.all_gather(both, "row", axis=0)
    all_a = got[:, :, :whole].reshape(row_count // 2, 2, tokens, whole)
    all_b = got[:, :, whole:].reshape(row_count // 2, tokens, HEAD)
    heads = jnp.concatenate([all_a[:, 0], all_b, all_a[:, 1]], axis=2)
    heads = heads.transpose(1, 0, 2).reshape(tokens, D)
    projected = contract_last(heads, out_block)
    residual = own.astype(jnp.float32) * mask
    return (residual + projected).astype(jnp.bfloat16)


def solution(mesh):
    in_specs = (
        P(None, "row"),
        P(),
        P(),
        P(),
        P(None, ("row", "col"), None),
        P(),
        P(None, ("row", "col"), None),
    )
    out_specs = P("col", "row")
    return jax.shard_map(
        per_device, mesh=mesh, in_specs=in_specs, out_specs=out_specs, check_vma=False
    )
```

time: 527 us -> 513 us (0.973)
  blocking collectives: 69.7 us -> 0 us
  waiting for transfers between devices: 330 us -> 385 us
  local copies, waits for them, and re-layouts: 48.7 us -> 54.6 us
  starting transfers between devices: 6.57 us -> 1.2 us
    all_gather x2 -> x4, waiting for transfers between devices: 145 us -> 385 us  [the longest x1 187 us: per_device(): block = lax.all_gather(merged[:3], 'col', axis=1, tiled=True)]
    reduce_scatter x1 -> x0, waiting for transfers between devices: 108 us -> none  [per_device(): lax.psum_scatter(contract_last(all_heads, out_block).astype(jnp.bfloat16)...]
    all_to_all x1 -> x0, waiting for transfers between devices: 77.2 us -> none  [per_device(): lax.all_to_all(hidden_states, 'row', split_axis=0, concat_axis=1, tiled=T...]
    all_to_all x3 -> x0, blocking collectives: 69.7 us -> none  [the longest x1 29.6 us: per_device(): lax.all_to_all(lax.all_to_all(merged_weights[:3], 'row', split_axis=2, co...]
    transpose x0 -> x2, local copies, waits for them, and re-layouts: none -> 17.3 us  [the longest x1 15.2 us: per_device(): heads = heads.transpose(1, 0, 2).reshape(tokens, D)]
    unnamed x20 -> x22, local copies, waits for them, and re-layouts: 18.8 us -> 2.7 us
    all_to_all x4 -> x0, local copies, waits for them, and re-layouts: 12.7 us -> none  [the longest x2 7.29 us: per_device(): lax.all_to_all(merged_weights[:3], 'row', split_axis=2, concat_axis=1, ti...]
    convert_element_type x5 -> x0, other arithmetic: 12.1 us -> none  [the longest x1 7.16 us: normalize(): ((embedded - average) * lax.rsqrt(variance + ln_eps) * gain_part + bias_p...]
  transfers between devices with their start and end apart: 4 -> 5, of which waited for: 4 -> 4; matrix products, arithmetic and copies ran while one was open for 3% -> 13% of each run, Pallas kernels for 0% -> 0%
where the time goes in v1:
time: 513 us; the launch traced here: 512 us
  waiting for transfers between devices  385 us (75%)
  local copies, waits for them, and re-layouts  54.6 us (11%)
  matrix products  40.8 us (8%)
  other arithmetic  17 us (3%)
  between operations  13.5 us (3%)
    all_gather x1, waiting for transfers between devices, per_device(): block = lax.all_gather(merged[:3], 'col', axis=1, tiled=True)  187 us
    all_gather x1, waiting for transfers between devices, per_device(): got = lax.all_gather(both, 'row', axis=0)  89.7 us
    all_gather x1, waiting for transfers between devices, per_device(): states = lax.all_gather(own, 'row', axis=1, tiled=True)  76.2 us
    all_gather x1, waiting for transfers between devices, per_device(): out_block = lax.all_gather(merged[3], 'col', axis=0, tiled=True)  31.8 us
    dot_general x2, matrix products, contract_last(): lax.dot_general(left_rows, right_rows, (((1,), (1,)), ((), ())), preferre...  29.9 us
    transpose x1, local copies, waits for them, and re-layouts, per_device(): heads = heads.transpose(1, 0, 2).reshape(tokens, D)  15.2 us
  transfers between devices with their start and end apart: 5, of which 4 were waited for; matrix products, arithmetic and copies ran while one was open for 13% of the time, Pallas kernels for 0%

profile of v1, /device:TPU:1, one launch (start us, length us, event | category | flops | bytes accessed | tf_op | source)
XLA Modules:
  0.0 511.8 jit_solution(11128873028591384837)
XLA Ops:
  6.5 2.0 constant_dynamic-slice_fusion.2
  8.6 6.8 %fusion.7 = bf16[4,40,5120]{2,1,0:T(8,128)(2,1)S(1)} fusion(f32[4,40,5120]{2,1,0:T(8,128)} %param.11, f32[4,40,64]{2,1,0:T(8,128)S(1)} %copy-done, f32[4,64,5120]{2,1,0:T(8,128)} %param.12), kind=kOutput, calls=%fused_computation.11 | convolution fusion | flops 631603200 | bytes 10199040 | tf_op jit(solution)/shard_map/dvc,dcw->dvw/dot_general | solution.py:74
  15.5 1.2 copy-done.2
  16.7 1.1 slice.89
  18.4 0.5 fusion.48
  19.1 76.2 %all-gather.7.cloned.1.call-done = bf16[1024,5120]{0,1:T(8,128)(2,1)} async-done(((bf16[1024,320]{0,1:T(8,128)(2,1)}), bf16[1024,5120]{0,1:T(8,128)(2,1)}) %all-gather.7.cloned.1.call-update) | async-done | bytes 10485776 | tf_op jit(solution)/shard_map/all_gather | solution.py:70
  95.2 7.4 %fusion.2 = (f32[1024]{0:T(1024)S(1)}, f32[1024]{0:T(1024)S(1)}) fusion(bf16[1024,5120]{0,1:T(8,128)(2,1)} %all-gather.7.cloned.1.call-done, f32[1024]{0:T(1024)S(1)} %bitcast.79), kind=kLoop, calls=%fused_computation.5 | loop fusion | flops 26212352 | bytes 10498048 | tf_op jit(solution)/shard_map/reduce_sum | solution.py:89
  102.7 187.0 %all-gather.9.cloned.1.call-done = bf16[3,320,5120]{2,1,0:T(8,128)(2,1)} async-done(((bf16[3,40,5120]{2,1,0:T(8,128)(2,1)}), bf16[3,320,5120]{2,1,0:T(8,128)(2,1)}) %all-gather.9.cloned.1.call-update) | async-done | bytes 9830416 | tf_op jit(solution)/shard_map/all_gather | solution.py:84
  289.7 20.5 %fusion.4 = f32[1024,3,320]{0,2,1:T(8,128)} fusion(bf16[3,320,5120]{2,1,0:T(8,128)(2,1)} %all-gather.9.cloned.1.call-done, bf16[1024,5120]{0,1:T(8,128)(2,1)} %all-gather.7.cloned.1.call-done, f32[5120]{0:T(1024)S(1)} %copy-done.7, f32[5120]{0:T(1024)S(1)} %copy-done.8, f32[1024]{0:T(1024)S(1)} %get-tuple-element.26, f32[1024]{0:T(1024)S(1)} %get-tuple-element.25, ...), kind=kOutput, calls=%fused_computation.8 | convolution fusion | flops 10103029760 | bytes 24301568 | tf_op jit(solution)/shard_map/dot_general | solution.py:30
  310.2 2.1 dynamic-slice_bitcast_fusion
  312.4 1.1 fusion.58
  313.5 2.4 constant_dynamic-slice_fusion.1
  315.9 0.6 collective-permute-start
  317.4 1.2 convert_element_type.83
  318.6 1.7 squeeze.28
  320.7 0.7 slice_negate_fusion
  321.4 0.8 fusion.30
  322.3 1.3 copy-done.4
  323.6 0.7 fusion.61
  324.3 2.6 fusion.19
  327.4 1.2 fusion.29
  330.3 1.0 pad_maximum_fusion
  331.7 1.8 slice.88
  333.5 89.7 %all-gather.11.cloned.1.call-done = bf16[16384,320]{1,0:T(8,128)(2,1)} async-done(((bf16[1024,320]{1,0:T(8,128)(2,1)}), bf16[16384,320]{1,0:T(8,128)(2,1)}) %all-gather.11.cloned.1.call-update) | async-done | bytes 10485776 | tf_op jit(solution)/shard_map/all_gather | solution.py:114
  423.1 4.6 slice.106
  427.8 7.3 %slice.104 = bf16[16,1024,256]{2,1,0:T(8,128)(2,1)} slice(bf16[16,1024,320]{2,1,0:T(8,128)(2,1)} %bitcast.71), slice={[0:16], [0:1024], [0:256]} | slice | bytes 16777216 | tf_op jit(solution)/shard_map/slice | solution.py:115
  435.1 5.1 reshape.191
  440.2 3.8 slice_bitcast_fusion.1
  444.0 4.8 maximum_bitcast_fusion
  448.8 15.2 %copy.66 = bf16[1024,8,640]{0,2,1:T(8,128)(2,1)} copy(bf16[1024,8,640]{2,0,1:T(8,128)(2,1)} %maximum_bitcast_fusion) | data formatting | bytes 20971520 | tf_op jit(solution)/shard_map/transpose | solution.py:118
  464.0 31.8 %all-gather.13.cloned.1.call-done = bf16[1,320,5120]{2,1,0:T(8,128)(2,1)} async-done(((bf16[1,40,5120]{2,1,0:T(8,128)(2,1)}), bf16[1,320,5120]{2,1,0:T(8,128)(2,1)}) %all-gather.13.cloned.1.call-update) | async-done | bytes 3276816 | tf_op jit(solution)/shard_map/all_gather | solution.py:85
  495.8 9.4 %fusion.14 = bf16[1024,320]{0,1:T(8,128)(2,1)} fusion(bf16[1024,5120]{0,1:T(8,128)(2,1)} %bitcast.72, bf16[1,320,5120]{2,1,0:T(8,128)(2,1)} %all-gather.13.cloned.1.call-done, bf16[1024,320]{0,1:T(8,128)(2,1)S(1)} %copy-done.3, f32[1024]{0:T(1024)S(1)} %bitcast.81), kind=kOutput, calls=%fused_computation.22 | convolution fusion | flops 3356753920 | bytes 15077376 | tf_op jit(solution)/shard_map/dot_general | solution.py:30
  (52 shorter events, 4.5 us)
Async XLA Ops:
  6.5 2.1 copy-start
  6.5 88.7 %all-gather.7.cloned.1.call-start = ((), (), s32[]{:S(2)}) async-start(), calls=%async_computation | async-start | bytes 11141120 | tf_op jit(solution)/shard_map/all_gather | solution.py:70
  8.6 9.6 %copy-start.9 = (s32[32]{0:T(128)S(1)}, s32[32]{0:T(128)}, u32[]{:S(2)}) copy-start(s32[32]{0:T(128)} %param.8) | copy-start | bytes 388
  8.6 281.1 %all-gather.9.cloned.1.call-start = ((), (), s32[]{:S(2)}) async-start(), calls=%async_computation.1 | async-start | bytes 11059200 | tf_op jit(solution)/shard_map/all_gather | solution.py:84
  15.4 1.3 copy-start.2
  17.9 405.3 %all-gather.11.cloned.1.call-start = ((), (), s32[]{:S(2)}) async-start(), calls=%async_computation.2 | async-start | bytes 13369344 | tf_op jit(solution)/shard_map/all_gather | solution.py:114
  95.2 194.4 %copy-start.7 = (f32[5120]{0:T(1024)S(1)}, f32[5120]{0:T(1024)}, u32[]{:S(2)}) copy-start(f32[5120]{0:T(1024)} %param.10) | copy-start | bytes 61444
  95.2 194.4 %copy-start.8 = (f32[5120]{0:T(1024)S(1)}, f32[5120]{0:T(1024)}, u32[]{:S(2)}) copy-start(f32[5120]{0:T(1024)} %param.9) | copy-start | bytes 61444
  315.9 11.5 %collective-permute-start = (f32[512,3,64]{0,2,1:T(8,128)}, f32[512,3,64]{0,2,1:T(8,128)}, u32[]{:S(2)}, u32[]{:S(2)}) collective-permute-start(f32[512,3,64]{0,2,1:T(8,128)} %get-tuple-element.10), channel_id=1, source_target_pairs={{0,8},{8,0},{16,24},{24,16},{32,40},{40,32},{48,56},{56,48},{64,72... | collective-permute-start | bytes 1179656 | tf_op jit(solution)/shard_map/ppermute | solution.py:101
  321.4 2.8 copy-start.6
  322.2 1.3 copy-start.4
  324.3 3.1 copy-start.5
  331.4 164.5 %all-gather.13.cloned.1.call-start = ((), (), s32[]{:S(2)}) async-start(), calls=%async_computation.3 | async-start | bytes 3686400 | tf_op jit(solution)/shard_map/all_gather | solution.py:85
  448.8 47.0 %copy-start.3 = (bf16[1024,320]{0,1:T(8,128)(2,1)S(1)}, bf16[1024,320]{0,1:T(8,128)(2,1)}, u32[]{:S(2)}) copy-start(bf16[1024,320]{0,1:T(8,128)(2,1)} %constant_dynamic-slice_fusion.2) | copy-start | bytes 1966084
  495.8 9.4 %copy-start.1 = (f32[4,40,64]{2,1,0:T(8,128)S(1)}, f32[4,40,64]{2,1,0:T(8,128)}, u32[]{:S(2)}) copy-start(f32[4,40,64]{2,1,0:T(8,128)} %param.13) | copy-start | bytes 122884
Sparse Core Ops, SparseCore 0:
  9.8 85.3 all-gather.6
  96.9 192.7 all-gather.8
  331.5 91.6 all-gather.10
  424.6 71.1 all-gather.12

commit v2 on v1

v2 whole, which is shorter than its diff:
```python
import functools

import jax
import jax.numpy as jnp
from jax import lax
from jax.experimental import pallas as pl
from jax.experimental.pallas import tpu as pltpu
from jax.sharding import PartitionSpec as P

MESH = pl.DeviceIdType.MESH
D = 5120
HEAD = 128
HALF = 64
LEN = 256

adapter_scale = 2.0
ln_eps = 1e-05

def plan(do_t, do_w, t_rows, t_cols, w_rows, w_cols, w_first, t_chunk, w_chunk):
    todo = []

    def add(key, link, size, dep, rank):
        todo.append(dict(key=key, link=link, size=size, dep=dep, rank=rank))

    if do_t:
        n = t_rows // t_chunk
        size = t_chunk * t_cols * 2
        for ch in range(n):
            first, second = ("xl", "cross") if ch < n // 2 else ("cross", "xl")
            add(("t", "hop", 0, 0, ch), first, size, None, 0)
            add(("t", "far", 0, 0, ch), second, size, ("t", "hop", 0, 0, ch), 0)
            for other in (0, 1):
                dep = None if other == 0 else ("t", "far", 0, 0, ch)
                for step in (1, -1):
                    add(("t", "ring", step, other, ch), ("y", step), size, dep, other)
                step = 1 if ch < n // 2 else -1
                add(("t", "pass", step, other, ch), ("y", step), size, ("t", "ring", step, other, ch), 2 + other)
                add(("t", "pair", 0, other, ch), "core", size, dep, 0)
                for step in (1, -1):
                    add(("t", "pair", step, other, ch), "core", size, ("t", "ring", step, other, ch), 0)
                step = 1 if ch < n // 2 else -1
                add(("t", "pair", 2, other, ch), "core", size, ("t", "pass", step, other, ch), 0)
    if do_w:
        n = w_rows // w_chunk
        for ch in range(n):
            step2 = 1 if ch < n // 2 else -1
            size = w_chunk * w_first * 2
            if w_first:
                for step in (1, -1):
                    add(("p", "ring", step, 0, ch), ("z", step), size, None, 1)
                    add(("p", "x", step, 0, ch), "xl", size, ("p", "ring", step, 0, ch), 1)
                add(("p", "pass", step2, 0, ch), ("z", step2), size, ("p", "ring", step2, 0, ch), 2)
                add(("p", "x", 0, 0, ch), "xl", size, None, 1)
                add(("p", "x", 2, 0, ch), "xl", size, ("p", "pass", step2, 0, ch), 2)
            size = w_chunk * (w_cols - w_first) * 2
            add(("s", "x", 0, 0, ch), "xl", size, None, 0)
            for other in (0, 1):
                dep = None if other == 0 else ("s", "x", 0, 0, ch)
                for step in (1, -1):
                    add(("s", "ring", step, other, ch), ("z", step), size, dep, other)
                add(("s", "pass", step2, other, ch), ("z", step2), size, ("s", "ring", step2, other, ch), 2 + other)

    arrive = {None: 0.0}
    free = {}
    events = []
    left = list(todo)
    while left:
        best = None
        for t in left:
            if t["dep"] in arrive:
                start = max(arrive[t["dep"]] + 1.0, free.get(t["link"], 0.0))
                score = (start, t["rank"])
                if best is None or score < best[0]:
                    best = (score, t, start)
        _, t, start = best
        rate = 300e3 if t["link"] == "core" else 50e3
        end = start + t["size"] / rate
        free[t["link"]] = end
        arrive[t["key"]] = end
        events.append((start, t))
        left.remove(t)
    return events, arrive


def gather_kernel(cfg, *refs):
    do_t, do_w = cfg["do_t"], cfg["do_w"]
    refs = list(refs)
    t_ref = refs.pop(0) if do_t else None
    w_ref = refs.pop(0) if do_w else None
    t_all = refs.pop(0) if do_t else None
    w_all = refs.pop(0) if do_w else None
    send, recv, local = refs[:3]
    relay = refs[3] if do_t else None
    row, col = lax.axis_index("row"), lax.axis_index("col")
    xh, y, core = row // 8, row // 2 % 4, row % 2
    z, xl = col // 2, col % 2

    def at(dxh=0, dy=0, dcore=0, dz=0, dxl=0):
        r = (xh + dxh) % 2 * 8 + (y + dy + 4) % 4 * 2 + (core + dcore) % 2
        c = (z + dz + 4) % 4 * 2 + (xl + dxl) % 2
        return r, c

    events, arrive = plan(**cfg)
    t_chunk, w_chunk, w_first = cfg["t_chunk"], cfg["w_chunk"], cfg["w_first"]
    peers = []
    if do_t:
        peers += [at(dxh=1, dxl=1), at(dy=1), at(dy=-1), at(dcore=1)]
    if do_w:
        peers += [at(dz=1), at(dz=-1)]
    peers += [at(dxl=1)]
    barrier = pltpu.get_barrier_semaphore()
    for peer in peers:
        pl.semaphore_signal(barrier, inc=1, device_id=peer, device_id_type=MESH)
    own = []
    if do_t:
        own.append(pltpu.make_async_copy(t_ref, t_all.at[row], local.at[0]))
    if do_w:
        own.append(pltpu.make_async_copy(w_ref, w_all.at[col], local.at[1]))
    for c in own:
        c.start()
    pl.semaphore_wait(barrier, len(peers))

    copies = {}
    waited = set()

    def make(i, t):
        kind, what, step, other, ch = t["key"]
        if kind == "t":
            rows = pl.ds(ch * t_chunk, t_chunk)
            one, two = at(dxl=1), at(dxh=1, dxl=1)
            if ch >= cfg["t_rows"] // t_chunk // 2:
                one, two = two, one
            if what == "hop":
                return pltpu.make_async_remote_copy(
                    src_ref=t_ref.at[rows], dst_ref=relay.at[rows], send_sem=send.at[i],
                    recv_sem=recv.at[i], device_id=one, device_id_type=MESH,
                )
            if what == "far":
                slot = at() if ch < cfg["t_rows"] // t_chunk // 2 else at(dxh=1)
                return pltpu.make_async_remote_copy(
                    src_ref=relay.at[rows], dst_ref=t_all.at[slot[0], rows], send_sem=send.at[i],
                    recv_sem=recv.at[i], device_id=two, device_id_type=MESH,
                )
            elif what == "ring":
                slot, to = at(dxh=other), at(dy=step)
            elif what == "pass":
                slot, to = at(dxh=other, dy=-step), at(dy=step)
            else:
                slot, to = at(dxh=other, dy=-step), at(dcore=1)
            mine = what == "ring" and other == 0 or what == "pair" and step == 0 and other == 0
            dst = t_all.at[slot[0], rows]
            src = t_ref.at[rows] if mine else dst
        else:
            rows = pl.ds(ch * w_chunk, w_chunk)
            cols = pl.ds(0, w_first) if kind == "p" else pl.ds(w_first, cfg["w_cols"] - w_first)
            if what == "x":
                slot, to = at(dz=-step), at(dxl=1)
            elif what == "ring":
                slot, to = at(dxl=other), at(dz=step)
            else:
                slot, to = at(dxl=other, dz=-step), at(dz=step)
            mine = other == 0 and (what == "ring" or what == "x" and step == 0)
            dst = w_all.at[slot[1], rows, cols]
            src = w_ref.at[rows, cols] if mine else dst
        return pltpu.make_async_remote_copy(
            src_ref=src, dst_ref=dst, send_sem=send.at[i], recv_sem=recv.at[i],
            device_id=to, device_id_type=MESH,
        )

    for i, (_, t) in enumerate(events):
        dep = t["dep"]
        if dep is not None and dep not in waited:
            copies[dep].wait_recv()
            waited.add(dep)
        copies[t["key"]] = make(i, t)
        copies[t["key"]].start()
    for key in sorted(copies, key=lambda k: arrive[k]):
        if key not in waited:
            copies[key].wait_recv()
    for key in copies:
        copies[key].wait_send()
    for c in own:
        c.wait()


def gather(t, w, w_first, t_chunk=80, w_chunk=32, collective_id=0):
    do_t, do_w = t is not None, w is not None
    cfg = dict(
        do_t=do_t, do_w=do_w,
        t_rows=t.shape[0] if do_t else 0, t_cols=t.shape[1] if do_t else 0,
        w_rows=w.shape[0] if do_w else 0, w_cols=w.shape[1] if do_w else 0,
        w_first=w_first, t_chunk=t_chunk, w_chunk=w_chunk,
    )
    count = len(plan(**cfg)[0])
    out = []
    if do_t:
        out.append(jax.ShapeDtypeStruct((16,) + t.shape, t.dtype))
    if do_w:
        out.append(jax.ShapeDtypeStruct((8,) + w.shape, w.dtype))
    args = [a for a in (t, w) if a is not None]
    return pl.pallas_call(
        functools.partial(gather_kernel, cfg),
        out_shape=out,
        in_specs=[pl.BlockSpec(memory_space=pl.ANY)] * len(args),
        out_specs=[pl.BlockSpec(memory_space=pl.ANY)] * len(args),
        scratch_shapes=[
            pltpu.SemaphoreType.DMA((count,)),
            pltpu.SemaphoreType.DMA((count,)),
            pltpu.SemaphoreType.DMA((2,)),
        ] + ([pltpu.VMEM(t.shape, t.dtype)] if do_t else []),
        compiler_params=pltpu.CompilerParams(collective_id=collective_id, has_side_effects=True),
    )(*args)


def rotary_tables(length, head_dim):
    half_dim = head_dim // 2
    frequency = 10000.0 ** (-(2.0 * jnp.arange(half_dim, dtype=jnp.float32)) / head_dim)
    angles = jnp.arange(length, dtype=jnp.float32)[:, None] * frequency[None, :]
    angles = jnp.concatenate([angles, angles], axis=1)
    return (jnp.cos(angles), jnp.sin(angles))


def attend(qkv, lengths, cosine, sine):
    def rotate(u):
        turned = jnp.concatenate([-u[:, HALF:], u[:, :HALF]], axis=1)
        return (u * cosine[None, :, None] + turned * sine[None, :, None]).astype(jnp.bfloat16)

    queries, key_rows, value_rows = rotate(qkv[0]), rotate(qkv[1]), qkv[2].astype(jnp.bfloat16)
    scores = jnp.einsum(
        "hdpq,hdpk->hpkq", queries, key_rows, preferred_element_type=jnp.float32
    ) * HEAD ** (-0.5)
    key_valid = jnp.arange(LEN, dtype=jnp.int32)[None, :] < lengths[:, None]
    scores = jnp.where(key_valid[None, :, :, None], scores, -jnp.inf)
    exponent = jnp.exp(scores - jnp.max(scores, axis=2, keepdims=True))
    soft = (exponent / jnp.sum(exponent, axis=2, keepdims=True)).astype(jnp.bfloat16)
    out = jnp.einsum("hpkq,hdpk->hdpq", soft, value_rows, preferred_element_type=jnp.float32)
    return out.astype(jnp.bfloat16).reshape(out.shape[0] * HEAD, -1)


def per_device(
    hidden_states,
    lengths,
    layer_norm_gain,
    layer_norm_bias,
    weights,
    adapter_down_factors,
    adapter_up_factors,
):
    col_count = lax.axis_size("col")
    row_count = lax.axis_size("row")
    row_idx = lax.axis_index("row")
    col_idx = lax.axis_index("col")
    core = row_idx % 2
    tokens = hidden_states.shape[0] // col_count
    proteins = tokens // LEN
    own = lax.dynamic_slice_in_dim(hidden_states, col_idx * tokens, tokens, 0)
    merged = (
        weights
        + adapter_scale
        * jnp.einsum(
            "dvc,dcw->dvw",
            adapter_up_factors,
            adapter_down_factors,
            precision=lax.Precision.HIGHEST,
        )
    ).astype(jnp.bfloat16)
    shard = merged.shape[1]
    merged = merged.reshape(4 * shard, D)
    states, block = gather(own.T, merged[:128], 1664, 160, 64, collective_id=0)
    local_lengths = lax.dynamic_slice_in_dim(lengths, col_idx * proteins, proteins, 0)
    valid = (jnp.arange(LEN, dtype=jnp.int32)[None, :] < local_lengths[:, None]).reshape(tokens)
    mask = valid[None, :].astype(jnp.float32)

    embedded = states.reshape(D, tokens).astype(jnp.float32) * mask
    average = jnp.sum(embedded, axis=0)[None, :] / D
    variance = jnp.sum(embedded * embedded, axis=0)[None, :] / D - average * average
    normed = (
        (embedded - average) * lax.rsqrt(variance + ln_eps) * layer_norm_gain[:, None]
        + layer_norm_bias[:, None]
    ).astype(jnp.bfloat16)
    out = jnp.dot(block.reshape(col_count * 128, D), normed, preferred_element_type=jnp.float32)
    out = out.reshape(col_count, 128, tokens)
    part = col_count * shard
    qkv = out[:, : 3 * shard].reshape(col_count, 3, shard, tokens)
    qkv = qkv.transpose(1, 0, 2, 3).reshape(3, part, tokens)
    whole = part // HEAD * HEAD
    mine = lax.dynamic_slice_in_dim(qkv, core * HALF, whole, 1)
    half = lax.dynamic_slice_in_dim(qkv, (1 - core) * whole, HALF, 1)
    half_tokens = tokens // 2
    keep = lax.dynamic_slice_in_dim(half, core * half_tokens, half_tokens, 2)
    send = lax.dynamic_slice_in_dim(half, (1 - core) * half_tokens, half_tokens, 2)
    got = lax.ppermute(send, "row", [(i, i ^ 1) for i in range(row_count)])
    split = jnp.where(
        core == 0,
        jnp.concatenate([keep, got], axis=1),
        jnp.concatenate([got, keep], axis=1),
    )
    cosine, sine = rotary_tables(LEN, HEAD)
    cosine, sine = cosine.T, sine.T
    mine = mine.reshape(3, whole // HEAD, HEAD, proteins, LEN)
    split = split.reshape(3, 1, HEAD, proteins // 2, LEN)
    split_lengths = lax.dynamic_slice_in_dim(local_lengths, core * (proteins // 2), proteins // 2, 0)
    attn_a = attend(mine, local_lengths, cosine, sine)
    attn_b = attend(split, split_lengths, cosine, sine)
    attn_b = jnp.concatenate([attn_b[:HALF], attn_b[HALF:]], axis=1)
    both = jnp.concatenate([attn_a, attn_b], axis=0)
    got, rest = gather(both, merged[128:], 1664, 160, 16, collective_id=1)
    all_a = got[:, :whole].reshape(row_count // 2, 2, whole, tokens)
    all_b = got[:, whole:].reshape(row_count // 2, 2, HALF, 2, half_tokens)
    all_b = all_b.transpose(0, 3, 2, 1, 4).reshape(row_count // 2, HEAD, tokens)
    heads = jnp.concatenate([all_a[:, 0], all_b, all_a[:, 1]], axis=1).reshape(D, tokens)
    out_block = jnp.concatenate([block[:, 3 * shard :], rest], axis=1).reshape(part, D)
    projected = jnp.dot(out_block, heads, preferred_element_type=jnp.float32).T
    residual = own.astype(jnp.float32) * mask[0][:, None]
    return (residual + projected).astype(jnp.bfloat16)


def solution(mesh):
    in_specs = (
        P(None, "row"),
        P(),
        P(),
        P(),
        P(None, ("row", "col"), None),
        P(),
        P(None, ("row", "col"), None),
    )
    out_specs = P("col", "row")
    return jax.shard_map(
        per_device, mesh=mesh, in_specs=in_specs, out_specs=out_specs, check_vma=False
    )
```

time: 513 us -> 238 us (0.46)
  waiting for transfers between devices: 385 us -> 0.01 us
  Pallas kernels: 0 us -> 131 us
  between operations: 13.5 us -> 0.38 us
  local copies, waits for them, and re-layouts: 54.6 us -> 44.6 us
  other arithmetic: 17 us -> 26.8 us
  matrix products: 40.8 us -> 31 us
    all_gather x4 -> x0, waiting for transfers between devices: 385 us -> none  [the longest x1 187 us: per_device(): block = lax.all_gather(merged[:3], 'col', axis=1, tiled=True)]
    pallas_call x0 -> x2, Pallas kernels: none -> 131 us  [gather(): pl.pallas_call(functools.partial(gather_kernel, cfg), out_shape=out, in_s...]
    transpose x2 -> x3, local copies, waits for them, and re-layouts: 17.3 us -> 2.15 us  [the longest x1 1.96 us: per_device(): states, block = gather(own.T, merged[:128], 1664, 160, 64, collective_id=0)]
    dot_general x6 -> x5, matrix products: 33.9 us -> 21 us  [the longest x1 12.9 us: per_device(): jnp.dot(block.reshape(col_count * 128, D), normed, preferred_element_type...]
    concatenate x2 -> x4, other arithmetic: 1.24 us -> 10.2 us  [the longest x1 8.84 us: per_device(): jnp.concatenate([all_a[:, 0], all_b, all_a[:, 1]], axis=1)]
    convert_element_type x0 -> x2, other arithmetic: none -> 6.39 us  [the longest x1 4.85 us: per_device(): normed = ((embedded - average) * lax.rsqrt(variance + ln_eps) * layer_nor...]
    reshape x1 -> x4, local copies, waits for them, and re-layouts: 5.06 us -> 11.3 us  [the longest x2 7.79 us: per_device(): all_b = got[:, whole:].reshape(row_count // 2, 2, HALF, 2, half_tokens)]
    transpose x2 -> x1, other arithmetic: 6.03 us -> 0.46 us  [per_device(): cosine, sine = (cosine.T, sine.T)]
  transfers between devices with their start and end apart: 5 -> 1, of which waited for: 4 -> 0; matrix products, arithmetic and copies ran while one was open for 13% -> 7% of each run, Pallas kernels for 0% -> 0%
where the time goes in v2:
time: 238 us; the launch traced here: 237 us
  Pallas kernels  131 us (55%)
  local copies, waits for them, and re-layouts  44.6 us (19%)
  matrix products  31 us (13%)
  other arithmetic  26.8 us (11%)
  starting transfers between devices  2.79 us (1%)
    pallas_call x2, Pallas kernels, gather(): pl.pallas_call(functools.partial(gather_kernel, cfg), out_shape=out, in_s...  131 us
    dot_general x1, matrix products, per_device(): jnp.dot(block.reshape(col_count * 128, D), normed, preferred_element_type...  12.9 us
    concatenate x1, other arithmetic, per_device(): jnp.concatenate([all_a[:, 0], all_b, all_a[:, 1]], axis=1)  8.84 us
    slice x1, local copies, waits for them, and re-layouts, per_device(): all_a = got[:, :whole].reshape(row_count // 2, 2, whole, tokens)  8.04 us
    reshape x2, local copies, waits for them, and re-layouts, per_device(): all_b = got[:, whole:].reshape(row_count // 2, 2, HALF, 2, half_tokens)  7.79 us
    reduce_sum x1, other arithmetic, per_device(): average = jnp.sum(embedded, axis=0)[None, :] / D  7.58 us
    dot_general x1, matrix products, per_device(): jnp.einsum('dvc,dcw->dvw', adapter_up_factors, adapter_down_factors, prec...  6.8 us
    dot_general x1, matrix products, per_device(): projected = jnp.dot(out_block, heads, preferred_element_type=jnp.float32).T  5.55 us
  transfers between devices with their start and end apart: 1, of which 0 were waited for; matrix products, arithmetic and copies ran while one was open for 7% of the time, Pallas kernels for 0%

profile of v2, /device:TPU:1, one launch (start us, length us, event | category | flops | bytes accessed | tf_op | source)
XLA Modules:
  0.0 237.0 jit_solution(4961143334047515735)
XLA Ops:
  0.8 0.8 mul.202
  1.6 0.8 add.83
  2.4 6.8 %fusion.6 = bf16[4,40,5120]{2,1,0:T(8,128)(2,1)S(1)} fusion(f32[4,40,5120]{2,1,0:T(8,128)} %param.11, f32[4,40,64]{2,1,0:T(8,128)S(1)} %copy-done, f32[4,64,5120]{2,1,0:T(8,128)} %param.12), kind=kOutput, calls=%fused_computation.11 | convolution fusion | flops 631603200 | bytes 10199040 | tf_op jit(solution)/shard_map/dvc,dcw->dvw/dot_general | solution.py:260
  9.3 1.2 copy-done.4
  10.4 1.2 slice.113.refs_1_
  11.6 2.0 dynamic-slice_bitcast_fusion.refs_0_
  13.6 78.7 %shard_map.73 = (bf16[16,320,1024]{2,1,0:T(8,128)(2,1)}, bf16[8,128,5120]{2,1,0:T(8,128)(2,1)}) custom-call(bf16[320,1024]{1,0:T(8,128)(2,1)} %dynamic-slice_bitcast_fusion.refs_0_, bf16[128,5120]{1,0:T(8,128)(2,1)} %slice.113.refs_1_), custom_call_target="tpu_custom_call" | custom-call | tf_op jit(solution)/shard_map/pallas_call | solution.py:201
  92.3 7.6 %fusion.2 = (f32[1024]{0:T(1024)S(1)}, f32[1024]{0:T(1024)S(1)}) fusion(bf16[16,320,1024]{2,1,0:T(8,128)(2,1)} %get-tuple-element.10, f32[1024]{0:T(1024)S(1)} %bitcast.87), kind=kLoop, calls=%fused_computation.5 | loop fusion | flops 26212352 | bytes 10498048 | tf_op jit(solution)/shard_map/reduce_sum | solution.py:275
  99.9 4.9 %add_convert_fusion = bf16[16,320,1024]{2,1,0:T(8,128)(2,1)S(1)} fusion(bf16[16,320,1024]{2,1,0:T(8,128)(2,1)S(1)} %copy-done.2, f32[16,320]{1,0:T(8,128)S(1)} %add.83, f32[16,320]{1,0:T(8,128)S(1)} %mul.202, f32[1024]{0:T(1024)S(1)} %get-tuple-element.38, f32[1024]{0:T(1024)S(1)} %get-tuple-element.37, f32[1024]{0:T(1024)S(1)} %bitcast.88), kind=kLoop, calls=%fused_computation.2 | loop fusion | flops 36700160 | bytes 21024768 | tf_op jit(solution)/shard_map/convert_element_type | solution.py:280
  104.8 12.9 %fusion.3 = f32[8,120,1024]{2,1,0:T(8,128)S(1)} fusion(bf16[5120,1024,1]{1,0,2:T(8,128)(2,1)S(1)} %bitcast.69, bf16[8,128,5120]{2,1,0:T(8,128)(2,1)} %get-tuple-element.9), kind=kOutput, calls=%fused_computation.7 | convolution fusion | flops 10066329600 | bytes 24248320 | tf_op jit(solution)/shard_map/dot_general | solution.py:281
  118.0 2.0 copy-done.3
  120.0 1.2 constant_dynamic-slice_fusion.2
  121.1 2.8 %collective-permute-start = (f32[3,64,512]{2,1,0:T(8,128)}, f32[3,64,512]{2,1,0:T(8,128)}, u32[]{:S(2)}, u32[]{:S(2)}) collective-permute-start(f32[3,64,512]{2,1,0:T(8,128)} %get-tuple-element.20), channel_id=1, source_target_pairs={{0,8},{8,0},{16,24},{24,16},{32,40},{40,32},{48,56},{56,48},{64,72... | collective-permute-start | bytes 1179656 | tf_op jit(solution)/shard_map/ppermute | solution.py:292
  124.5 1.3 dynamic-slice_convert_fusion
  125.8 1.2 convert_element_type.94
  127.0 1.7 constant_dynamic-slice_fusion
  130.1 1.5 fusion.15
  131.7 3.2 %fusion.58 = (f32[2,4,256]{2,1,0:T(4,128)S(1)}, f32[2,4,256,256]{3,2,1,0:T(8,128)}) fusion(pred[4,256]{1,0:T(4,128)(4,1)S(1)} %get-tuple-element.39, bf16[2,128,4,256]{3,2,1,0:T(4,128)(2,1)} %get-tuple-element.28, bf16[2,128,4,256]{3,2,1,0:T(4,128)(2,1)S(1)} %get-tuple-element.27), kind=kOutput, calls=%fused_computation.88 | convolution fusion | flops 136315136 | bytes 3154944 | tf_op jit(solution)/shard_map/sub | solution.py:234
  134.9 1.9 fusion.11
  137.0 1.7 slice.127.refs_1_
  138.8 1.1 slice.111
  140.6 1.3 maximum_select_fusion
  143.6 0.9 maximum_maximum_fusion.refs_0_
  144.4 52.6 %shard_map.74 = (bf16[16,320,1024]{2,1,0:T(8,128)(2,1)}, bf16[8,32,5120]{2,1,0:T(8,128)(2,1)}) custom-call(bf16[320,1024]{1,0:T(8,128)(2,1)} %maximum_maximum_fusion.refs_0_, bf16[32,5120]{1,0:T(8,128)(2,1)} %slice.127.refs_1_), custom_call_target="tpu_custom_call" | custom-call | tf_op jit(solution)/shard_map/pallas_call | solution.py:201
  197.1 1.9 slice.109
  199.0 8.0 %slice.107 = bf16[16,256,1024]{2,1,0:T(8,128)(2,1)} slice(bf16[16,320,1024]{2,1,0:T(8,128)(2,1)} %get-tuple-element.11), slice={[0:16], [0:256], [0:1024]} | slice | bytes 16777216 | tf_op jit(solution)/shard_map/slice | solution.py:308
  207.0 2.7 %reshape.261 = bf16[8,2,64,2,512]{4,3,2,1,0:T(2,128)(2,1)} reshape(bf16[16,64,1024]{2,1,0:T(8,128)(2,1)S(1)} %slice.109) | data formatting | bytes 4194304 | tf_op jit(solution)/shard_map/reshape | solution.py:309
  209.7 5.1 %copy.68 = bf16[8,2,64,2,512]{4,1,2,3,0:T(2,128)(2,1)} copy(bf16[8,2,64,2,512]{4,3,2,1,0:T(2,128)(2,1)} %reshape.261) | data formatting | bytes 4194304 | tf_op jit(solution)/shard_map/reshape | solution.py:309
  214.8 3.2 %reshape.262 = bf16[8,128,1024]{2,1,0:T(8,128)(2,1)S(1)} reshape(bf16[8,2,64,2,512]{4,3,2,1,0:T(2,128)(2,1)} %bitcast.71) | data formatting | bytes 4194304 | tf_op jit(solution)/shard_map/reshape | solution.py:310
  218.0 4.1 %slice_bitcast_fusion.1 = (bf16[8,256,1024]{2,1,0:T(8,128)(2,1)S(1)}, bf16[8,256,1024]{2,1,0:T(8,128)(2,1)S(1)}) fusion(bf16[8,2,256,1024]{3,2,1,0:T(8,128)(2,1)} %bitcast.65), kind=kLoop, calls=%fused_computation.13 | loop fusion | bytes 16777216 | tf_op jit(solution)/shard_map/squeeze | solution.py:311
  222.5 8.8 %pad_maximum_fusion = bf16[8,640,1024]{2,1,0:T(8,128)(2,1)S(1)} fusion(bf16[8,256,1024]{2,1,0:T(8,128)(2,1)S(1)} %get-tuple-element.16, bf16[8,128,1024]{2,1,0:T(8,128)(2,1)S(1)} %reshape.262, bf16[8,256,1024]{2,1,0:T(8,128)(2,1)S(1)} %get-tuple-element.15), kind=kLoop, calls=%fused_computation.6 | loop fusion | flops 31457280 | bytes 20971520 | tf_op jit(solution)/shard_map/concatenate | solution.py:311
  231.4 5.6 %fusion.8 = bf16[1024,320]{0,1:T(8,128)(2,1)} fusion(bf16[320,5120]{1,0:T(8,128)(2,1)S(1)} %bitcast.79, bf16[5120,1024]{1,0:T(8,128)(2,1)S(1)} %bitcast.70, f32[1024]{0:T(1024)S(1)} %bitcast.89, bf16[8192,320]{0,1:T(8,128)(2,1)} %param.7, s32[]{:T(128)S(6)} %select_n.55), kind=kOutput, calls=%fused_computation.21 | convolution fusion | flops 3356753920 | bytes 15077380 | tf_op jit(solution)/shard_map/dot_general | solution.py:313
  (49 shorter events, 5.9 us)
Async XLA Ops:
  0.0 2.4 %copy-start = (f32[4,40,64]{2,1,0:T(8,128)S(1)}, f32[4,40,64]{2,1,0:T(8,128)}, u32[]{:S(2)}) copy-start(f32[4,40,64]{2,1,0:T(8,128)} %param.13) | copy-start | bytes 122884
  9.3 1.2 copy-start.4
  92.3 7.6 %copy-start.2 = (bf16[16,320,1024]{2,1,0:T(8,128)(2,1)S(1)}, bf16[16,320,1024]{2,1,0:T(8,128)(2,1)}, u32[]{:S(2)}) copy-start(bf16[16,320,1024]{2,1,0:T(8,128)(2,1)} %get-tuple-element.10) | copy-start | bytes 31457284
  118.0 2.0 copy-start.3
  121.1 19.5 %collective-permute-start = (f32[3,64,512]{2,1,0:T(8,128)}, f32[3,64,512]{2,1,0:T(8,128)}, u32[]{:S(2)}, u32[]{:S(2)}) collective-permute-start(f32[3,64,512]{2,1,0:T(8,128)} %get-tuple-element.20), channel_id=1, source_target_pairs={{0,8},{8,0},{16,24},{24,16},{32,40},{40,32},{48,56},{56,48},{64,72... | collective-permute-start | bytes 1179656 | tf_op jit(solution)/shard_map/ppermute | solution.py:292
  130.1 4.8 %copy-start.7 = (bf16[2,128,4,256]{3,2,1,0:T(4,128)(2,1)S(1)}, bf16[2,128,4,256]{3,2,1,0:T(4,128)(2,1)}, u32[]{:S(2)}) copy-start(bf16[2,128,4,256]{3,2,1,0:T(4,128)(2,1)} %convert_element_type.94) | copy-start | bytes 1572868
  134.9 5.0 %copy-start.8 = (s32[32]{0:T(128)S(1)}, s32[32]{0:T(128)}, u32[]{:S(2)}) copy-start(s32[32]{0:T(128)} %param.8) | copy-start | bytes 388
  136.8 3.8 %copy-start.6 = (f32[3,64,512]{2,1,0:T(8,128)S(1)}, f32[3,64,512]{2,1,0:T(8,128)}, u32[]{:S(2)}) copy-start(f32[3,64,512]{2,1,0:T(8,128)} %get-tuple-element.19) | copy-start | bytes 1179652
  218.0 4.2 %copy-start.5 = (bf16[8,32,5120]{2,1,0:T(8,128)(2,1)S(1)}, bf16[8,32,5120]{2,1,0:T(8,128)(2,1)}, u32[]{:S(2)}) copy-start(bf16[8,32,5120]{2,1,0:T(8,128)(2,1)} %get-tuple-element.12) | copy-start | bytes 7864324
  231.4 5.6 %copy-start.1 = (f32[4,40,64]{2,1,0:T(8,128)S(1)}, f32[4,40,64]{2,1,0:T(8,128)}, u32[]{:S(2)}) copy-start(f32[4,40,64]{2,1,0:T(8,128)} %param.13) | copy-start | bytes 122884

commit v3 on v1

v3 whole, which is shorter than its diff:
```python
import functools

import jax
import jax.numpy as jnp
from jax import lax
from jax.experimental import pallas as pl
from jax.experimental.pallas import tpu as pltpu
from jax.sharding import PartitionSpec as P

MESH = pl.DeviceIdType.MESH
D = 5120
HEAD = 128
HALF = 64
LEN = 256
TOK = 1024
PART = 320
SHARD = 40
W1 = 128
W2 = 48
W2_FROM = 112
FIRST = 1664

adapter_scale = 2.0
ln_eps = 1e-05

T1_CHUNKS = [(0, 160), (160, 320)]
COLS = {"p": [(0, 768), (768, FIRST)], "s": [(FIRST, 3456), (3456, D)]}


def transfers():
    todo = []

    def add(key, link, size, deps, rank):
        todo.append(dict(key=key, link=link, size=size, deps=deps, rank=rank, time=None))

    def slots(kind, sizes, ready, rank):
        n = len(sizes)
        for ch, size in enumerate(sizes):
            up = ch < n // 2 if kind == "a" else ch % 2 == 0
            step2 = 1 if up else -1
            first, second = ("xl", "cross") if up else ("cross", "xl")
            start = ready(ch)
            add((kind, "hop", 0, 0, ch), first, size, start, rank)
            add((kind, "far", 0, 0, ch), second, size, [(kind, "hop", 0, 0, ch)], rank)
            for other in (0, 1):
                deps = start if other == 0 else [(kind, "far", 0, 0, ch)]
                for step in (1, -1):
                    add((kind, "ring", step, other, ch), ("y", step), size, deps, rank + other)
                ring = (kind, "ring", step2, other, ch)
                add((kind, "pass", step2, other, ch), ("y", step2), size, [ring], rank + 2 + other)
                add((kind, "pair", 0, other, ch), "core", size, deps, rank)
                for step in (1, -1):
                    add((kind, "pair", step, other, ch), "core", size, [(kind, "ring", step, other, ch)], rank)
                add((kind, "pair", 2, other, ch), "core", size, [(kind, "pass", step2, other, ch)], rank)

    def rows(kind, count, rank):
        for ch in (0, 1):
            step2 = 1 if ch == 0 else -1
            p, s = kind + "p", kind + "s"
            size = count * (COLS["p"][ch][1] - COLS["p"][ch][0]) * 2
            for step in (1, -1):
                add((p, "ring", step, 0, ch), ("z", step), size, [], rank + 1)
                add((p, "x", step, 0, ch), "xl", size, [(p, "ring", step, 0, ch)], rank + 1)
            add((p, "pass", step2, 0, ch), ("z", step2), size, [(p, "ring", step2, 0, ch)], rank + 2)
            add((p, "x", 0, 0, ch), "xl", size, [], rank + 1)
            add((p, "x", 2, 0, ch), "xl", size, [(p, "pass", step2, 0, ch)], rank + 2)
            size = count * (COLS["s"][ch][1] - COLS["s"][ch][0]) * 2
            add((s, "x", 0, 0, ch), "xl", size, [], rank)
            for other in (0, 1):
                deps = [] if other == 0 else [(s, "x", 0, 0, ch)]
                for step in (1, -1):
                    add((s, "ring", step, other, ch), ("z", step), size, deps, rank + other)
                ring = (s, "ring", step2, other, ch)
                add((s, "pass", step2, other, ch), ("z", step2), size, [ring], rank + 2 + other)

    slots("a", [(b - a) * TOK * 2 for a, b in T1_CHUNKS], lambda ch: [], 0)
    rows("v", W1, 1)
    rows("o", W2, 20)
    slots("b", [r * LEN * 2 for r in (256, 256, 384, 384)], lambda ch: [("attend", ch)], 10)
    for step in (0, 1):
        add(("h", "half", 0, 0, step), "core", 3 * HALF * LEN * 4, [("qkv", step)], -1)
    return todo


def step2_of(kind, ch):
    up = ch == 0 if kind == "a" else ch % 2 == 0
    return 1 if up else -1


def arrival(kind, step, other, ch):
    if step == 0:
        return [(kind, "far", 0, 0, ch)] if other else []
    if step == 2:
        return [(kind, "pass", step2_of(kind, ch), other, ch)]
    return [(kind, "ring", step, other, ch)]


def weight_keys(kind):
    return [t["key"] for t in transfers() if t["key"][0] in (kind + "p", kind + "s")]


def computes():
    todo = []

    def add(key, time, deps, rank, sends=()):
        todo.append(dict(key=key, time=time, deps=deps, rank=rank, sends=list(sends), link=None))

    spots = [(other, step) for other in (0, 1) for step in (0, 1, -1, 2)]
    stats = []
    for other, step in spots:
        for twin in (0, 1):
            deps = []
            for ch in range(len(T1_CHUNKS)):
                deps += [("a", "pair", step, other, ch)] if twin else arrival("a", step, other, ch)
            add(("stat", other, step, twin), 0.6, deps, 0)
            stats.append(("stat", other, step, twin))
    add(("moments",), 0.2, stats, 1)
    for other, step in spots:
        for twin in (0, 1):
            sends = []
            if not twin:
                for ch in range(len(T1_CHUNKS)):
                    if (other, step) != (0, 0):
                        sends.append(("a", "pair", step, other, ch))
                    if step == 0 and other == 1:
                        sends += [("a", "ring", 1, 1, ch), ("a", "ring", -1, 1, ch)]
                    if step == step2_of("a", ch):
                        sends.append(("a", "pass", step, other, ch))
            add(("norm", other, step, twin), 0.8, [("moments",)], 2, sends)
    norms = [("norm", o, s, t) for o, s in spots for t in (0, 1)]
    for s in range(4):
        add(("qkv", s), 3.2, norms + weight_keys("v"), 3 + s)
        deps = [("qkv", s)] + ([("h", "half", 0, 0, s - 2)] if s >= 2 else [])
        add(("attend", s), 1.5 if s < 2 else 2.2, deps, 2.5)
    for other, step in spots:
        for twin in (0, 1):
            for pair in (0, 1):
                deps = weight_keys("o")
                for ch in (2 * pair, 2 * pair + 1):
                    if twin:
                        deps += [("b", "pair", step, other, ch)]
                    elif (other, step) == (0, 0):
                        deps += [("attend", ch)]
                    else:
                        deps += arrival("b", step, other, ch)
                add(("out", other, step, twin, pair), 0.6, deps, 50)
    return todo


def schedule():
    left = transfers() + computes()
    done, free, order, now = {}, {}, [], 0.0
    while left:
        best, later = None, []
        for t in left:
            if not all(d in done for d in t["deps"]):
                continue
            ready = max([0.0] + [done[d] for d in t["deps"]])
            if t["link"] is not None:
                ready = max(ready, free.get(t["link"], 0.0) - 6.0)
            if ready > now:
                later.append(ready)
                continue
            score = (t["link"] is None, t["rank"])
            if best is None or score < best[0]:
                best = (score, t)
        if best is None:
            now = min(later)
            continue
        t = best[1]
        if t["link"] is None:
            now += t["time"]
            done[t["key"]] = now
        else:
            now += 0.1
            rate = 200e3 if t["link"] == "core" else 45e3
            end = max(now, free.get(t["link"], 0.0)) + t["size"] / rate
            free[t["link"]] = end
            done[t["key"]] = end + 1.5
        order.append(t)
        left.remove(t)
    return order, done


def fused(
    t_ref, w_ref, mask_ref, bias_ref, affine_ref, cos_ref, sin_ref, out_ref,
    t1, w1, w2, t2, relay1, relay2, qkv_s, half_s, sums, moments, acc, send, recv, local,
):
    row, col = lax.axis_index("row"), lax.axis_index("col")
    xh, y, core = row // 8, row // 2 % 4, row % 2
    z, xl = col // 2, col % 2

    def at(dxh=0, dy=0, dcore=0, dz=0, dxl=0):
        r = (xh + dxh) % 2 * 8 + (y + dy + 4) % 4 * 2 + (core + dcore) % 2
        c = (z + dz + 4) % 4 * 2 + (xl + dxl) % 2
        return r, c

    order, done = schedule()
    peers = [at(dy=1), at(dy=-1), at(dcore=1), at(dz=1), at(dz=-1), at(dxl=1), at(dxh=1, dxl=1)]
    barrier = pltpu.get_barrier_semaphore()
    for peer in peers:
        pl.semaphore_signal(barrier, inc=1, device_id=peer, device_id_type=MESH)
    own = [
        pltpu.make_async_copy(t_ref, t1.at[pl.ds(row * PART, PART)], local.at[0]),
        pltpu.make_async_copy(w_ref.at[pl.ds(0, W1)], w1.at[pl.ds(col * W1, W1)], local.at[1]),
        pltpu.make_async_copy(w_ref.at[pl.ds(W2_FROM, W2)], w2.at[pl.ds(col * W2, W2)], local.at[2]),
    ]
    for c in own:
        c.start()
    sums[...] = jnp.zeros_like(sums)
    acc[...] = jnp.zeros_like(acc)
    pl.semaphore_wait(barrier, len(peers))

    def protein(c, s):
        return (2 * (1 - c) + s) % 4

    def make(i, key):
        kind, what, step, other, ch = key

        def copy(src, dst, to):
            return pltpu.make_async_remote_copy(
                src_ref=src, dst_ref=dst, send_sem=send.at[i], recv_sem=recv.at[i],
                device_id=to, device_id_type=MESH,
            )

        if kind == "h":
            src = qkv_s.at[ch, :, pl.ds((1 - core) * 256, HALF), :]
            return copy(src, half_s.at[ch], at(dcore=1))
        if kind in ("a", "b"):
            def block(r):
                if kind == "a":
                    lo, hi = T1_CHUNKS[ch]
                    return t1.at[pl.ds(r * PART + lo, hi - lo)]
                return t2.at[r, ch, pl.ds(0, 256 if ch < 2 else 384)]

            def via():
                if kind == "a":
                    lo, hi = T1_CHUNKS[ch]
                    return relay1.at[pl.ds(lo, hi - lo)]
                return relay2.at[ch, pl.ds(0, 256 if ch < 2 else 384)]

            def source():
                if kind == "a":
                    lo, hi = T1_CHUNKS[ch]
                    return t_ref.at[pl.ds(lo, hi - lo)]
                return block(row)

            up = step2_of(kind, ch) == 1
            one, two = at(dxl=1), at(dxh=1, dxl=1)
            if not up:
                one, two = two, one
            if what == "hop":
                return copy(source(), via(), one)
            if what == "far":
                return copy(via(), block((at() if up else at(dxh=1))[0]), two)
            if what == "ring":
                slot, to = at(dxh=other), at(dy=step)
            elif what == "pass":
                slot, to = at(dxh=other, dy=-step), at(dy=step)
            else:
                slot, to = at(dxh=other, dy=-step), at(dcore=1)
            mine = other == 0 and (what == "ring" or what == "pair" and step == 0)
            return copy(source() if mine else block(slot[0]), block(slot[0]), to)
        lo, hi = COLS[kind[1]][ch]
        whole, count, first = (w1, W1, 0) if kind[0] == "v" else (w2, W2, W2_FROM)
        if what == "x":
            slot, to = at(dz=-step), at(dxl=1)
        elif what == "ring":
            slot, to = at(dxl=other), at(dz=step)
        else:
            slot, to = at(dxl=other, dz=-step), at(dz=step)
        mine = other == 0 and (what == "ring" or what == "x" and step == 0)
        dst = whole.at[pl.ds(slot[1] * count, count), pl.ds(lo, hi - lo)]
        src = w_ref.at[pl.ds(first, count), pl.ds(lo, hi - lo)] if mine else dst
        return copy(src, dst, to)

    def slot_of(other, step, twin):
        return at(dxh=other, dy=-step, dcore=twin)[0]

    def stat(other, step, twin):
        base = slot_of(other, step, twin) * PART

        def body(i, carry):
            one, two = carry
            x = t1[pl.ds(pl.multiple_of(base + i * 16, 16), 16), :].astype(jnp.float32) * mask_ref[...]
            return one + x[:8] + x[8:], two + x[:8] * x[:8] + x[8:] * x[8:]

        one, two = lax.fori_loop(0, PART // 16, body, (sums[0], sums[1]))
        sums[0] = one
        sums[1] = two

    def get_moments():
        average = jnp.sum(sums[0], axis=0, keepdims=True) / D
        variance = jnp.sum(sums[1], axis=0, keepdims=True) / D - average * average
        moments[0] = average
        moments[1] = lax.rsqrt(variance + ln_eps)

    def norm(other, step, twin):
        base = slot_of(other, step, twin) * PART

        def body(i, carry):
            here = pl.ds(pl.multiple_of(base + i * 16, 16), 16)
            x = t1[here, :].astype(jnp.float32) * mask_ref[...]
            gain = affine_ref[here, 0:1]
            shift = affine_ref[here, 1:2]
            t1[here, :] = ((x - moments[0]) * moments[1] * gain + shift).astype(jnp.bfloat16)
            return carry

        lax.fori_loop(0, PART // 16, body, 0)

    def qkv(s):
        lanes = pl.ds(pl.multiple_of(protein(core, s) * LEN, LEN), LEN)
        for m in range(2):
            result = jnp.dot(
                w1[pl.ds(m * 512, 512), :], t1[:, lanes], preferred_element_type=jnp.float32
            )
            for j in range(4):
                for k in range(3):
                    qkv_s[s, k, pl.ds((m * 4 + j) * SHARD, SHARD), :] = result[
                        j * W1 + k * SHARD : j * W1 + (k + 1) * SHARD
                    ]

    def head(first, second, keys, s, rows):
        cosine, sine = cos_ref[...], sin_ref[...]

        def rotate(k):
            u, v = first[k], second[k]
            return jnp.concatenate([u * cosine - v * sine, v * cosine + u * sine], axis=0).astype(jnp.bfloat16)

        queries, key_rows = rotate(0), rotate(1)
        value_rows = jnp.concatenate([first[2], second[2]], axis=0).astype(jnp.bfloat16)
        scores = lax.dot_general(
            key_rows, queries, (((0,), (0,)), ((), ())), preferred_element_type=jnp.float32
        ) * HEAD ** (-0.5)
        scores = scores + keys
        exponent = jnp.exp(scores - jnp.max(scores, axis=0, keepdims=True))
        soft = (exponent * (1.0 / jnp.sum(exponent, axis=0, keepdims=True))).astype(jnp.bfloat16)
        got = jnp.dot(value_rows, soft, preferred_element_type=jnp.float32)
        t2[row, s, pl.ds(rows, HEAD), :] = got.astype(jnp.bfloat16)

    def attend(s):
        keys = bias_ref[pl.ds(pl.multiple_of(protein(core, s) * LEN, LEN), LEN), :]
        for h in range(2):
            start = core * HALF + h * HEAD
            first = [qkv_s[s, k, pl.ds(pl.multiple_of(start, HALF), HALF), :] for k in range(3)]
            second = [qkv_s[s, k, pl.ds(pl.multiple_of(start + HALF, HALF), HALF), :] for k in range(3)]
            head(first, second, keys, s, h * HEAD)
        if s >= 2:
            first, second = [], []
            for k in range(3):
                mine = qkv_s[s, k, pl.ds(pl.multiple_of((1 - core) * 256, HALF), HALF), :]
                came = half_s[s - 2, k]
                first.append(jnp.where(core == 0, mine, came))
                second.append(jnp.where(core == 0, came, mine))
            head(first, second, keys, s, 256)

    def project(other, step, twin, pair):
        r = slot_of(other, step, twin)
        chip, c = r // 2, r % 2
        cols = pl.ds(pl.multiple_of(chip * 640 + c * 384, 128), 256)
        middle = pl.ds(pl.multiple_of(chip * 640 + 256, 128), 128)
        for s in (2 * pair, 2 * pair + 1):
            p = protein(c, s)
            value = jnp.dot(w2[:, cols], t2[r, s, 0:256, :], preferred_element_type=jnp.float32)
            if pair:
                value += jnp.dot(w2[:, middle], t2[r, s, 256:384, :], preferred_element_type=jnp.float32)
            acc[p] += value

    copies, waited, gone = {}, set(), set()
    local_done = [False]
    for i, t in enumerate(order):
        key = t["key"]
        for dep in t["deps"]:
            if dep in copies and dep not in waited:
                copies[dep].wait_recv()
                waited.add(dep)
        if t["link"] is not None:
            copies[key] = make(len(copies), key)
            copies[key].start()
            continue
        if not local_done[0]:
            for c in own:
                c.wait()
            local_done[0] = True
        for dep in t["sends"]:
            copies[dep].wait_send()
            gone.add(dep)
        dict(stat=stat, moments=get_moments, norm=norm, qkv=qkv, attend=attend, out=project)[key[0]](*key[1:])
    for key in sorted(copies, key=lambda k: done[k]):
        if key not in waited:
            copies[key].wait_recv()
        if key not in gone:
            copies[key].wait_send()
    for j in range(4):
        for p in range(4):
            value = jnp.concatenate(
                [acc[p, pl.ds(96 * j + 8, SHARD), :], acc[p, pl.ds(96 * j + 56, SHARD), :]], axis=0
            )
            lanes = pl.ds(p * LEN, LEN)
            rest = t_ref[pl.ds(80 * j, 80), lanes].astype(jnp.float32) * mask_ref[:, lanes]
            out_ref[pl.ds(80 * j, 80), lanes] = (rest + value).astype(jnp.bfloat16)


def run_fused(states, merged, mask, bias, affine, cosine, sine):
    count = len(transfers())
    vmem = pl.BlockSpec(memory_space=pltpu.VMEM)
    return pl.pallas_call(
        fused,
        out_shape=jax.ShapeDtypeStruct((PART, TOK), jnp.bfloat16),
        in_specs=[vmem] * 7,
        out_specs=vmem,
        scratch_shapes=[
            pltpu.VMEM((D, TOK), jnp.bfloat16),
            pltpu.VMEM((8 * W1, D), jnp.bfloat16),
            pltpu.VMEM((8 * W2, D), jnp.bfloat16),
            pltpu.VMEM((16, 4, 384, LEN), jnp.bfloat16),
            pltpu.VMEM((PART, TOK), jnp.bfloat16),
            pltpu.VMEM((4, 384, LEN), jnp.bfloat16),
            pltpu.VMEM((4, 3, PART, LEN), jnp.float32),
            pltpu.VMEM((2, 3, HALF, LEN), jnp.float32),
            pltpu.VMEM((2, 8, TOK), jnp.float32),
            pltpu.VMEM((2, 1, TOK), jnp.float32),
            pltpu.VMEM((4, 8 * W2, LEN), jnp.float32),
            pltpu.SemaphoreType.DMA((count,)),
            pltpu.SemaphoreType.DMA((count,)),
            pltpu.SemaphoreType.DMA((3,)),
        ],
        compiler_params=pltpu.CompilerParams(
            collective_id=0, has_side_effects=True, vmem_limit_bytes=60 * 1024 * 1024
        ),
    )(states, merged, mask, bias, affine, cosine, sine)


def rotary_tables():
    half_dim = HEAD // 2
    frequency = 10000.0 ** (-(2.0 * jnp.arange(half_dim, dtype=jnp.float32)) / HEAD)
    angles = frequency[:, None] * jnp.arange(LEN, dtype=jnp.float32)[None, :]
    return jnp.cos(angles), jnp.sin(angles)


def per_device(
    hidden_states,
    lengths,
    layer_norm_gain,
    layer_norm_bias,
    weights,
    adapter_down_factors,
    adapter_up_factors,
):
    col_idx = lax.axis_index("col")
    own = lax.dynamic_slice_in_dim(hidden_states, col_idx * TOK, TOK, 0)
    merged = (
        weights
        + adapter_scale
        * jnp.einsum(
            "dvc,dcw->dvw",
            adapter_up_factors,
            adapter_down_factors,
            precision=lax.Precision.HIGHEST,
        )
    ).astype(jnp.bfloat16)
    merged = merged.reshape(4 * SHARD, D)
    proteins = TOK // LEN
    local_lengths = lax.dynamic_slice_in_dim(lengths, col_idx * proteins, proteins, 0)
    valid = (jnp.arange(LEN, dtype=jnp.int32)[None, :] < local_lengths[:, None]).reshape(TOK)
    mask = valid[None, :].astype(jnp.float32)
    bias = jnp.where(valid, 0.0, -jnp.inf).astype(jnp.float32)[:, None]
    affine = jnp.stack([layer_norm_gain, layer_norm_bias], axis=1)
    cosine, sine = rotary_tables()
    return run_fused(own.T, merged, mask, bias, affine, cosine, sine).T


def solution(mesh):
    in_specs = (
        P(None, "row"),
        P(),
        P(),
        P(),
        P(None, ("row", "col"), None),
        P(),
        P(None, ("row", "col"), None),
    )
    out_specs = P("col", "row")
    return jax.shard_map(
        per_device, mesh=mesh, in_specs=in_specs, out_specs=out_specs, check_vma=False
    )
```

time: 513 us -> 164 us (0.32)
  waiting for transfers between devices: 385 us -> 0 us
  Pallas kernels: 0 us -> 145 us
  local copies, waits for them, and re-layouts: 54.6 us -> 8.65 us
  matrix products: 40.8 us -> 7.96 us
  other arithmetic: 17 us -> 1.91 us
  between operations: 13.5 us -> 0.02 us
    all_gather x4 -> x0, waiting for transfers between devices: 385 us -> none  [the longest x1 187 us: per_device(): block = lax.all_gather(merged[:3], 'col', axis=1, tiled=True)]
    pallas_call x0 -> x1, Pallas kernels: none -> 145 us  [run_fused(): pl.pallas_call(fused, out_shape=jax.ShapeDtypeStruct((PART, TOK), jnp.bfl...]
    dot_general x6 -> x0, matrix products: 33.9 us -> none  [the longest x2 29.9 us: contract_last(): lax.dot_general(left_rows, right_rows, (((1,), (1,)), ((), ())), preferre...]
    slice x8 -> x0, local copies, waits for them, and re-layouts: 16.1 us -> none  [the longest x1 7.33 us: per_device(): all_a = got[:, :, :whole].reshape(row_count // 2, 2, tokens, whole)]
    transpose x2 -> x1, local copies, waits for them, and re-layouts: 17.3 us -> 1.96 us  [per_device(): return run_fused(own.T, merged, mask, bias, affine, cosine, sine).T]
    reduce_sum x1 -> x0, other arithmetic: 7.44 us -> none  [per_device(): average = jnp.sum(embedded, axis=1)[:, None] / D]
    squeeze x7 -> x0, local copies, waits for them, and re-layouts: 7.04 us -> none  [the longest x1 3.82 us: per_device(): heads = jnp.concatenate([all_a[:, 0], all_b, all_a[:, 1]], axis=2)]
    transpose x2 -> x0, other arithmetic: 6.03 us -> none  [the longest x1 4.81 us: per_device(): heads = heads.transpose(1, 0, 2).reshape(tokens, D)]
  transfers between devices with their start and end apart: 5 -> 0, of which waited for: 4 -> 0; matrix products, arithmetic and copies ran while one was open for 13% -> 0% of each run, Pallas kernels for 0% -> 0%
where the time goes in v3:
time: 164 us
  Pallas kernels  145 us (88%)
  local copies, waits for them, and re-layouts  8.65 us (5%)
  matrix products  7.96 us (5%)
  other arithmetic  1.91 us (1%)
    pallas_call x1, Pallas kernels, run_fused(): pl.pallas_call(fused, out_shape=jax.ShapeDtypeStruct((PART, TOK), jnp.bfl...  145 us
    dot_general x1, matrix products, per_device(): jnp.einsum('dvc,dcw->dvw', adapter_up_factors, adapter_down_factors, prec...  7.96 us
    unnamed x6, local copies, waits for them, and re-layouts  3.61 us

profile of v3, /device:TPU:1, one launch (start us, length us, event | category | flops | bytes accessed | tf_op | source)
XLA Modules:
  0.0 163.6 jit_solution(4210633837706041647)
XLA Ops:
  0.0 0.0 copy-start
  0.0 0.8 dynamic_slice.7
  0.8 0.1 select_bitcast_fusion
  0.9 0.1 convert_bitcast_fusion
  0.9 0.6 copy.13
  1.5 0.8 pad_maximum_fusion
  2.3 1.0 fusion.2
  3.3 1.0 copy.15
  4.3 2.0 %dynamic-slice_bitcast_fusion.t_ref = bf16[320,1024]{1,0:T(8,128)(2,1)} fusion(bf16[8192,320]{0,1:T(8,128)(2,1)} %param.7, s32[]{:T(128)S(6)} %select_n.20), kind=kLoop, calls=%fused_computation.3 | loop fusion | bytes 1310724 | tf_op jit(solution)/shard_map/transpose | solution.py:470
  6.3 0.0 copy-done
  6.3 8.0 %fusion.1 = bf16[4,40,5120]{2,1,0:T(8,128)(2,1)} fusion(f32[4,40,5120]{2,1,0:T(8,128)} %param.11, f32[4,40,64]{2,1,0:T(8,128)S(1)} %copy-done, f32[4,64,5120]{2,1,0:T(8,128)} %param.12), kind=kOutput, calls=%fused_computation.2 | convolution fusion | flops 631603200 | bytes 10199040 | tf_op jit(solution)/shard_map/dvc,dcw->dvw/dot_general | solution.py:455
  14.2 2.3 %copy.12.affine_ref = f32[5120,2]{1,0:T(8,128)} copy(f32[5120,2]{0,1:T(2,128)S(1)} %pad_maximum_fusion) | data formatting | bytes 81920 | tf_op jit(solution)/shard_map/stack | solution.py:468
  16.6 145.0 %shard_map.73 = bf16[320,1024]{1,0:T(8,128)(2,1)} custom-call(bf16[320,1024]{1,0:T(8,128)(2,1)} %dynamic-slice_bitcast_fusion.t_ref, bf16[160,5120]{1,0:T(8,128)(2,1)} %bitcast.17, f32[1,1024]{1,0:T(1,128)} %bitcast.23, f32[1024,1]{1,0:T(8,128)} %bitcast.19, f32[5120,2]{1,0:T(8,128)} %copy.12.affine_ref, f32[64,256]{1,0:T(8,128)} %get-tuple-element.6.cos_ref, ...), custom_call_target="tpu_custom_call" | custom-call | tf_op jit(solution)/shard_map/pallas_call | solution.py:407
  161.6 2.0 %copy.17 = bf16[1024,320]{0,1:T(8,128)(2,1)} copy(bf16[1024,320]{0,1:T(8,128)(2,1)} %bitcast.18) | data formatting | bytes 1310720
  (2 shorter events, 0.0 us)
Async XLA Ops:
  0.0 6.3 %copy-start = (f32[4,40,64]{2,1,0:T(8,128)S(1)}, f32[4,40,64]{2,1,0:T(8,128)}, u32[]{:S(2)}) copy-start(f32[4,40,64]{2,1,0:T(8,128)} %param.13) | copy-start | bytes 122884

commit v4 on v3

--- a/solution.py
+++ b/solution.py
@@ -2,11 +2,13 @@
 
 import jax
 import jax.numpy as jnp
+import numpy as np
 from jax import lax
 from jax.experimental import pallas as pl
 from jax.experimental.pallas import tpu as pltpu
 from jax.sharding import PartitionSpec as P
 
+VMEM_BYTES = 60 * 1024 * 1024
 MESH = pl.DeviceIdType.MESH
 D = 5120
 HEAD = 128
@@ -18,13 +20,16 @@
 W1 = 128
 W2 = 48
 W2_FROM = 112
-FIRST = 1664
 
 adapter_scale = 2.0
 ln_eps = 1e-05
 
 T1_CHUNKS = [(0, 160), (160, 320)]
-COLS = {"p": [(0, 768), (768, FIRST)], "s": [(FIRST, 3456), (3456, D)]}
+
+
+COLS = {"p": [(0, 768), (768, 1792)], "s": [(1792, 3584), (3584, D)]}
+LATE = (3,)
+SLACK = 3.0
 
 
 def transfers():
@@ -40,10 +45,20 @@
             step2 = 1 if up else -1
             first, second = ("xl", "cross") if up else ("cross", "xl")
             start = ready(ch)
+            late = kind == "b" and ch in LATE
             add((kind, "hop", 0, 0, ch), first, size, start, rank)
             add((kind, "far", 0, 0, ch), second, size, [(kind, "hop", 0, 0, ch)], rank)
             for other in (0, 1):
                 deps = start if other == 0 else [(kind, "far", 0, 0, ch)]
+                if late and other:
+                    add((kind, "pair", 0, 1, ch), "core", size, deps, rank)
+                    for step in (1, -1, 2):
+                        first, second = second, first
+                        came = (kind, "pass" if step == 2 else "ring", step2 if step == 2 else step, 0, ch)
+                        add((kind, "hop", step, 0, ch), first, size, [came], rank + 1)
+                        add((kind, "far", step, 0, ch), second, size, [(kind, "hop", step, 0, ch)], rank + 1)
+                        add((kind, "pair", step, 1, ch), "core", size, [(kind, "far", step, 0, ch)], rank)
+                    continue
                 for step in (1, -1):
                     add((kind, "ring", step, other, ch), ("y", step), size, deps, rank + other)
                 ring = (kind, "ring", step2, other, ch)
@@ -57,17 +72,18 @@
         for ch in (0, 1):
             step2 = 1 if ch == 0 else -1
             p, s = kind + "p", kind + "s"
+            own_p, own_s = [("merge", "p", ch)], [("merge", "s", ch)]
             size = count * (COLS["p"][ch][1] - COLS["p"][ch][0]) * 2
             for step in (1, -1):
-                add((p, "ring", step, 0, ch), ("z", step), size, [], rank + 1)
+                add((p, "ring", step, 0, ch), ("z", step), size, own_p, rank + 1)
                 add((p, "x", step, 0, ch), "xl", size, [(p, "ring", step, 0, ch)], rank + 1)
             add((p, "pass", step2, 0, ch), ("z", step2), size, [(p, "ring", step2, 0, ch)], rank + 2)
-            add((p, "x", 0, 0, ch), "xl", size, [], rank + 1)
+            add((p, "x", 0, 0, ch), "xl", size, own_p, rank + 1)
             add((p, "x", 2, 0, ch), "xl", size, [(p, "pass", step2, 0, ch)], rank + 2)
             size = count * (COLS["s"][ch][1] - COLS["s"][ch][0]) * 2
-            add((s, "x", 0, 0, ch), "xl", size, [], rank)
+            add((s, "x", 0, 0, ch), "xl", size, own_s, rank)
             for other in (0, 1):
-                deps = [] if other == 0 else [(s, "x", 0, 0, ch)]
+                deps = own_s if other == 0 else [(s, "x", 0, 0, ch)]
                 for step in (1, -1):
                     add((s, "ring", step, other, ch), ("z", step), size, deps, rank + other)
                 ring = (s, "ring", step2, other, ch)
@@ -90,6 +106,8 @@
 def arrival(kind, step, other, ch):
     if step == 0:
         return [(kind, "far", 0, 0, ch)] if other else []
+    if other and kind == "b" and ch in LATE:
+        return [(kind, "far", step, 0, ch)]
     if step == 2:
         return [(kind, "pass", step2_of(kind, ch), other, ch)]
     return [(kind, "ring", step, other, ch)]
@@ -106,15 +124,20 @@
         todo.append(dict(key=key, time=time, deps=deps, rank=rank, sends=list(sends), link=None))
 
     spots = [(other, step) for other in (0, 1) for step in (0, 1, -1, 2)]
+    for part in "sp":
+        for ch in (0, 1):
+            lo, hi = COLS[part][ch]
+            add(("merge", part, ch), 1.2 + 4.0 * (hi - lo) / D, [], -1)
+    add(("columns",), 2.0, [], -0.5)
     stats = []
     for other, step in spots:
         for twin in (0, 1):
             deps = []
             for ch in range(len(T1_CHUNKS)):
                 deps += [("a", "pair", step, other, ch)] if twin else arrival("a", step, other, ch)
-            add(("stat", other, step, twin), 0.6, deps, 0)
+            add(("stat", other, step, twin), 0.6, deps + [("columns",)], 0)
             stats.append(("stat", other, step, twin))
-    add(("moments",), 0.2, stats, 1)
+    add(("moments",), 0.2, stats + [("columns",)], 1)
     for other, step in spots:
         for twin in (0, 1):
             sends = []
@@ -149,6 +172,10 @@
 
 def schedule():
     left = transfers() + computes()
+    for t in left:
+        rate = 200e3 if t["link"] == "core" else 45e3
+        if t["link"] is not None:
+            t["time"] = t["size"] / rate
     done, free, order, now = {}, {}, [], 0.0
     while left:
         best, later = None, []
@@ -157,7 +184,7 @@
                 continue
             ready = max([0.0] + [done[d] for d in t["deps"]])
             if t["link"] is not None:
-                ready = max(ready, free.get(t["link"], 0.0) - 6.0)
+                ready = max(ready, free.get(t["link"], 0.0) - SLACK)
             if ready > now:
                 later.append(ready)
                 continue
@@ -173,18 +200,16 @@
             done[t["key"]] = now
         else:
             now += 0.1
-            rate = 200e3 if t["link"] == "core" else 45e3
-            end = max(now, free.get(t["link"], 0.0)) + t["size"] / rate
-            free[t["link"]] = end
-            done[t["key"]] = end + 1.5
+            free[t["link"]] = max(now, free.get(t["link"], 0.0)) + t["time"]
+            done[t["key"]] = free[t["link"]] + 1.5
         order.append(t)
         left.remove(t)
     return order, done
 
 
 def fused(
-    t_ref, w_ref, mask_ref, bias_ref, affine_ref, cos_ref, sin_ref, out_ref,
-    t1, w1, w2, t2, relay1, relay2, qkv_s, half_s, sums, moments, acc, send, recv, local,
+    hidden_ref, w_ref, down_ref, lengths_ref, up_ref, gain_ref, shift_ref, cos_ref, sin_ref, out_ref,
+    t_ref, mask_ref, bias_ref, up_s, t1, w1, w2, t2, relay1, relay2, qkv_s, half_s, sums, moments, acc, w_f, down_f, affine, send, recv, local,
 ):
     row, col = lax.axis_index("row"), lax.axis_index("col")
     xh, y, core = row // 8, row // 2 % 4, row % 2
@@ -200,15 +225,46 @@
     barrier = pltpu.get_barrier_semaphore()
     for peer in peers:
         pl.semaphore_signal(barrier, inc=1, device_id=peer, device_id_type=MESH)
-    own = [
-        pltpu.make_async_copy(t_ref, t1.at[pl.ds(row * PART, PART)], local.at[0]),
-        pltpu.make_async_copy(w_ref.at[pl.ds(0, W1)], w1.at[pl.ds(col * W1, W1)], local.at[1]),
-        pltpu.make_async_copy(w_ref.at[pl.ds(W2_FROM, W2)], w2.at[pl.ds(col * W2, W2)], local.at[2]),
-    ]
-    for c in own:
+    mine = pltpu.make_async_copy(
+        hidden_ref.at[:, pl.ds(pl.multiple_of(col * TOK, TOK), TOK)], t_ref, local.at[0]
+    )
+    mine.start()
+    fetch = {}
+    for i, (part, ch) in enumerate(("s0", "s1", "p0", "p1")):
+        lo, hi = COLS[part][int(ch)]
+        cols = pl.ds(lo, hi - lo)
+        fetch[part, int(ch)] = [
+            pltpu.make_async_copy(w_ref.at[:, cols], w_f.at[:, cols], local.at[2 * i + 1]),
+            pltpu.make_async_copy(down_ref.at[:, cols], down_f.at[:, cols], local.at[2 * i + 2]),
+        ]
+    for c in sum(fetch.values(), []):
         c.start()
+
+    def pieces(x):
+        one = x.astype(jnp.bfloat16)
+        rest = x - one.astype(jnp.float32)
+        two = rest.astype(jnp.bfloat16)
+        return one, two, (rest - two.astype(jnp.float32)).astype(jnp.bfloat16)
+
+    def product(x, y):
+        return jnp.dot(x, y, preferred_element_type=jnp.float32)
+
+    def prepare_up():
+        rank = up_ref.shape[1]
+        r = lax.broadcasted_iota(jnp.int32, (rank, 4 * rank), 0)
+        c = lax.broadcasted_iota(jnp.int32, (rank, 4 * rank), 1)
+        spread = jnp.where(c % rank == r, 1.0, 0.0).astype(jnp.bfloat16)
+        r = lax.broadcasted_iota(jnp.int32, (4 * SHARD, 4 * rank), 0)
+        c = lax.broadcasted_iota(jnp.int32, (4 * SHARD, 4 * rank), 1) // rank * SHARD
+        inside = (r >= c) & (r < c + SHARD)
+        for i, piece in enumerate(pieces(up_ref[...] * adapter_scale)):
+            wide = jnp.where(inside, product(piece, spread), 0.0)
+            up_s[pl.ds(4 * SHARD * i, 4 * SHARD), :] = wide.astype(jnp.bfloat16)
+
     sums[...] = jnp.zeros_like(sums)
     acc[...] = jnp.zeros_like(acc)
+    prepare_up()
+    mine.wait()
     pl.semaphore_wait(barrier, len(peers))
 
     def protein(c, s):
@@ -237,6 +293,8 @@
                 if kind == "a":
                     lo, hi = T1_CHUNKS[ch]
                     return relay1.at[pl.ds(lo, hi - lo)]
+                if step:
+                    return relay2.at[3 + step % 4, pl.ds(0, 256 if ch < 2 else 384)]
                 return relay2.at[ch, pl.ds(0, 256 if ch < 2 else 384)]
 
             def source():
@@ -246,13 +304,15 @@
                 return block(row)
 
             up = step2_of(kind, ch) == 1
+            if step > 0 and what in ("hop", "far"):
+                up = not up
             one, two = at(dxl=1), at(dxh=1, dxl=1)
             if not up:
                 one, two = two, one
             if what == "hop":
-                return copy(source(), via(), one)
+                return copy(block(at(dy=-step)[0]) if step else source(), via(), one)
             if what == "far":
-                return copy(via(), block((at() if up else at(dxh=1))[0]), two)
+                return copy(via(), block(at(dxh=0 if up else 1, dy=-step)[0]), two)
             if what == "ring":
                 slot, to = at(dxh=other), at(dy=step)
             elif what == "pass":
@@ -262,22 +322,61 @@
             mine = other == 0 and (what == "ring" or what == "pair" and step == 0)
             return copy(source() if mine else block(slot[0]), block(slot[0]), to)
         lo, hi = COLS[kind[1]][ch]
-        whole, count, first = (w1, W1, 0) if kind[0] == "v" else (w2, W2, W2_FROM)
+        whole, count = (w1, W1) if kind[0] == "v" else (w2, W2)
         if what == "x":
             slot, to = at(dz=-step), at(dxl=1)
         elif what == "ring":
             slot, to = at(dxl=other), at(dz=step)
         else:
             slot, to = at(dxl=other, dz=-step), at(dz=step)
-        mine = other == 0 and (what == "ring" or what == "x" and step == 0)
         dst = whole.at[pl.ds(slot[1] * count, count), pl.ds(lo, hi - lo)]
-        src = w_ref.at[pl.ds(first, count), pl.ds(lo, hi - lo)] if mine else dst
-        return copy(src, dst, to)
+        return copy(dst, dst, to)
+
+    def merge(part, ch):
+        for c in fetch[part, ch]:
+            c.wait()
+
+        up = up_s[...]
+        rows = 4 * SHARD
+        lo, hi = COLS[part][ch]
+
+        def body(i, carry):
+            cols = pl.ds(pl.multiple_of(lo + i * 256, 256), 256)
+            one, two, three = pieces(down_f[:, cols])
+            a = product(up, one)
+            b = product(up[: 2 * rows], two)
+            total = a[2 * rows :] + b[rows:] + product(up[:rows], three)
+            total = total + (a[rows : 2 * rows] + b[:rows])
+            merged = (w_f[:, cols] + (total + a[:rows])).astype(jnp.bfloat16)
+            w1[pl.ds(pl.multiple_of(col * W1, W1), W1), cols] = merged[:W1]
+            w2[pl.ds(pl.multiple_of(col * W2, W2), W2), cols] = merged[W2_FROM:]
+            return carry
+
+        lax.fori_loop(0, (hi - lo) // 256, body, 0, unroll=True)
+
+    def columns():
+        lane = lax.broadcasted_iota(jnp.int32, lengths_ref.shape, 1)
+        for p in range(4):
+            length = jnp.sum(jnp.where(lane == col * 4 + p, lengths_ref[...], 0), axis=1, keepdims=True)
+            across = lax.broadcasted_iota(jnp.int32, (1, LEN), 1) < length
+            mask_ref[:, pl.ds(p * LEN, LEN)] = jnp.where(across, 1.0, 0.0)
+            down = lax.broadcasted_iota(jnp.int32, (LEN, 1), 0) < length
+            bias_ref[pl.ds(p * LEN, LEN), :] = jnp.where(down, 0.0, -jnp.inf)
+        for which, ref in enumerate((gain_ref, shift_ref)):
+            for j in range(D // 1024):
+                turned = ref[pl.ds(8 * j, 8), :].T
+                for i in range(8):
+                    affine[pl.ds((8 * j + i) * 128, 128), which : which + 1] = turned[:, i : i + 1]
 
     def slot_of(other, step, twin):
         return at(dxh=other, dy=-step, dcore=twin)[0]
 
+    def place():
+        t1[pl.ds(pl.multiple_of(row * PART, 16), PART), :] = t_ref[...]
+
     def stat(other, step, twin):
+        if (other, step, twin) == (0, 0, 0):
+            place()
         base = slot_of(other, step, twin) * PART
 
         def body(i, carry):
@@ -301,8 +400,8 @@
         def body(i, carry):
             here = pl.ds(pl.multiple_of(base + i * 16, 16), 16)
             x = t1[here, :].astype(jnp.float32) * mask_ref[...]
-            gain = affine_ref[here, 0:1]
-            shift = affine_ref[here, 1:2]
+            gain = affine[here, 0:1]
+            shift = affine[here, 1:2]
             t1[here, :] = ((x - moments[0]) * moments[1] * gain + shift).astype(jnp.bfloat16)
             return carry
 
@@ -367,7 +466,6 @@
             acc[p] += value
 
     copies, waited, gone = {}, set(), set()
-    local_done = [False]
     for i, t in enumerate(order):
         key = t["key"]
         for dep in t["deps"]:
@@ -378,14 +476,10 @@
             copies[key] = make(len(copies), key)
             copies[key].start()
             continue
-        if not local_done[0]:
-            for c in own:
-                c.wait()
-            local_done[0] = True
         for dep in t["sends"]:
             copies[dep].wait_send()
             gone.add(dep)
-        dict(stat=stat, moments=get_moments, norm=norm, qkv=qkv, attend=attend, out=project)[key[0]](*key[1:])
+        dict(merge=merge, columns=columns, stat=stat, moments=get_moments, norm=norm, qkv=qkv, attend=attend, out=project)[key[0]](*key[1:])
     for key in sorted(copies, key=lambda k: done[k]):
         if key not in waited:
             copies[key].wait_recv()
@@ -401,41 +495,48 @@
             out_ref[pl.ds(80 * j, 80), lanes] = (rest + value).astype(jnp.bfloat16)
 
 
-def run_fused(states, merged, mask, bias, affine, cosine, sine):
+def run_fused(*args):
     count = len(transfers())
-    vmem = pl.BlockSpec(memory_space=pltpu.VMEM)
+    vmem, hbm = pl.BlockSpec(memory_space=pltpu.VMEM), pl.BlockSpec(memory_space=pl.ANY)
     return pl.pallas_call(
         fused,
         out_shape=jax.ShapeDtypeStruct((PART, TOK), jnp.bfloat16),
-        in_specs=[vmem] * 7,
+        in_specs=[hbm] * 3 + [vmem] * 6,
         out_specs=vmem,
         scratch_shapes=[
+            pltpu.VMEM((PART, TOK), jnp.bfloat16),
+            pltpu.VMEM((1, TOK), jnp.float32),
+            pltpu.VMEM((TOK, 1), jnp.float32),
+            pltpu.VMEM((12 * SHARD, 256), jnp.bfloat16),
             pltpu.VMEM((D, TOK), jnp.bfloat16),
             pltpu.VMEM((8 * W1, D), jnp.bfloat16),
             pltpu.VMEM((8 * W2, D), jnp.bfloat16),
             pltpu.VMEM((16, 4, 384, LEN), jnp.bfloat16),
             pltpu.VMEM((PART, TOK), jnp.bfloat16),
-            pltpu.VMEM((4, 384, LEN), jnp.bfloat16),
+            pltpu.VMEM((7, 384, LEN), jnp.bfloat16),
             pltpu.VMEM((4, 3, PART, LEN), jnp.float32),
             pltpu.VMEM((2, 3, HALF, LEN), jnp.float32),
             pltpu.VMEM((2, 8, TOK), jnp.float32),
             pltpu.VMEM((2, 1, TOK), jnp.float32),
             pltpu.VMEM((4, 8 * W2, LEN), jnp.float32),
+            pltpu.VMEM((4 * SHARD, D), jnp.float32),
+            pltpu.VMEM((256, D), jnp.float32),
+            pltpu.VMEM((D, 2), jnp.float32),
             pltpu.SemaphoreType.DMA((count,)),
             pltpu.SemaphoreType.DMA((count,)),
-            pltpu.SemaphoreType.DMA((3,)),
+            pltpu.SemaphoreType.DMA((9,)),
         ],
         compiler_params=pltpu.CompilerParams(
-            collective_id=0, has_side_effects=True, vmem_limit_bytes=60 * 1024 * 1024
+            collective_id=0, has_side_effects=True, vmem_limit_bytes=VMEM_BYTES
         ),
-    )(states, merged, mask, bias, affine, cosine, sine)
+    )(*args)
 
 
 def rotary_tables():
     half_dim = HEAD // 2
-    frequency = 10000.0 ** (-(2.0 * jnp.arange(half_dim, dtype=jnp.float32)) / HEAD)
-    angles = frequency[:, None] * jnp.arange(LEN, dtype=jnp.float32)[None, :]
-    return jnp.cos(angles), jnp.sin(angles)
+    frequency = 10000.0 ** (-2.0 * np.arange(half_dim) / HEAD)
+    angles = frequency.astype(np.float32)[:, None] * np.arange(LEN, dtype=np.float32)[None, :]
+    return np.cos(angles).astype(np.float32), np.sin(angles).astype(np.float32)
 
 
 def per_device(
@@ -447,27 +548,20 @@
     adapter_down_factors,
     adapter_up_factors,
 ):
-    col_idx = lax.axis_index("col")
-    own = lax.dynamic_slice_in_dim(hidden_states, col_idx * TOK, TOK, 0)
-    merged = (
-        weights
-        + adapter_scale
-        * jnp.einsum(
-            "dvc,dcw->dvw",
-            adapter_up_factors,
-            adapter_down_factors,
-            precision=lax.Precision.HIGHEST,
-        )
-    ).astype(jnp.bfloat16)
-    merged = merged.reshape(4 * SHARD, D)
-    proteins = TOK // LEN
-    local_lengths = lax.dynamic_slice_in_dim(lengths, col_idx * proteins, proteins, 0)
-    valid = (jnp.arange(LEN, dtype=jnp.int32)[None, :] < local_lengths[:, None]).reshape(TOK)
-    mask = valid[None, :].astype(jnp.float32)
-    bias = jnp.where(valid, 0.0, -jnp.inf).astype(jnp.float32)[:, None]
-    affine = jnp.stack([layer_norm_gain, layer_norm_bias], axis=1)
+    rank = adapter_up_factors.shape[2]
     cosine, sine = rotary_tables()
-    return run_fused(own.T, merged, mask, bias, affine, cosine, sine).T
+    result = run_fused(
+        hidden_states.T,
+        weights.reshape(4 * SHARD, D),
+        adapter_down_factors.reshape(4 * rank, D),
+        lengths.reshape(1, -1),
+        adapter_up_factors.reshape(4 * SHARD, rank),
+        layer_norm_gain.reshape(D // 128, 128),
+        layer_norm_bias.reshape(D // 128, 128),
+        cosine,
+        sine,
+    )
+    return result.T
 
 
 def solution(mesh):

time: 164 us -> 152 us (0.927)
  matrix products: 7.96 us -> 0 us
  local copies, waits for them, and re-layouts: 8.65 us -> 1.97 us
  Pallas kernels: 145 us -> 150 us
  other arithmetic: 1.91 us -> 0 us
    dot_general x1 -> x0, matrix products: 7.96 us -> none  [per_device(): jnp.einsum('dvc,dcw->dvw', adapter_up_factors, adapter_down_factors, prec...]
    pallas_call x1, Pallas kernels: 145 us -> 150 us  [run_fused(): pl.pallas_call(fused, out_shape=jax.ShapeDtypeStruct((PART, TOK), jnp.bfl...]
    another operation x1 -> x0, local copies, waits for them, and re-layouts: 2.31 us -> none  [per_device(): affine = jnp.stack([layer_norm_gain, layer_norm_bias], axis=1)]
    transpose x1 -> x0, local copies, waits for them, and re-layouts: 1.96 us -> none  [per_device(): return run_fused(own.T, merged, mask, bias, affine, cosine, sine).T]
    unnamed x6 -> x1, local copies, waits for them, and re-layouts: 3.61 us -> 1.97 us
where the time goes in v4:
time: 152 us; the launch traced here: 151 us
  Pallas kernels  150 us (99%)
  local copies, waits for them, and re-layouts  1.97 us (1%)
    pallas_call x1, Pallas kernels, run_fused(): pl.pallas_call(fused, out_shape=jax.ShapeDtypeStruct((PART, TOK), jnp.bfl...  150 us

profile of v4, /device:TPU:1, one launch (start us, length us, event | category | flops | bytes accessed | tf_op | source)
XLA Modules:
  0.0 151.5 jit_solution(12132944465218220273)
XLA Ops:
  0.0 149.5 %shard_map.91 = bf16[320,1024]{1,0:T(8,128)(2,1)} custom-call(bf16[320,8192]{1,0:T(8,128)(2,1)} %bitcast.8, f32[160,5120]{1,0:T(8,128)} %bitcast.10, f32[256,5120]{1,0:T(8,128)} %bitcast.9, s32[1,32]{1,0:T(1,128)} %bitcast.15, f32[160,64]{1,0:T(8,128)} %bitcast.12, f32[40,128]{1,0:T(8,128)} %bitcast.13, f32[40,128]{1,0:T(8,128)} %bitcast.14, ...), custom_call_target="tpu_custom_call" | custom-call | tf_op jit(solution)/shard_map/pallas_call | solution.py:501
  149.5 2.0 %copy.11 = bf16[1024,320]{0,1:T(8,128)(2,1)} copy(bf16[1024,320]{0,1:T(8,128)(2,1)} %bitcast.11) | data formatting | bytes 1310720

commit v5 on v4

--- a/solution.py
+++ b/solution.py
@@ -30,6 +30,8 @@
 COLS = {"p": [(0, 768), (768, 1792)], "s": [(1792, 3584), (3584, D)]}
 LATE = (3,)
 SLACK = 3.0
+RATE = {"core": 100e3, "o": 30e3, "y": 40e3, "z": 42e3, "x": 40e3, "c": 40e3}
+LATENCY = 2.5
 
 
 def transfers():
@@ -91,7 +93,7 @@
 
     slots("a", [(b - a) * TOK * 2 for a, b in T1_CHUNKS], lambda ch: [], 0)
     rows("v", W1, 1)
-    rows("o", W2, 20)
+    rows("o", W2 - 16, 20)
     slots("b", [r * LEN * 2 for r in (256, 256, 384, 384)], lambda ch: [("attend", ch)], 10)
     for step in (0, 1):
         add(("h", "half", 0, 0, step), "core", 3 * HALF * LEN * 4, [("qkv", step)], -1)
@@ -155,10 +157,11 @@
         add(("qkv", s), 3.2, norms + weight_keys("v"), 3 + s)
         deps = [("qkv", s)] + ([("h", "half", 0, 0, s - 2)] if s >= 2 else [])
         add(("attend", s), 1.5 if s < 2 else 2.2, deps, 2.5)
+    add(("fill",), 0.4, weight_keys("v"), 40)
     for other, step in spots:
         for twin in (0, 1):
             for pair in (0, 1):
-                deps = weight_keys("o")
+                deps = weight_keys("o") + [("fill",)]
                 for ch in (2 * pair, 2 * pair + 1):
                     if twin:
                         deps += [("b", "pair", step, other, ch)]
@@ -170,10 +173,16 @@
     return todo
 
 
+def rate_of(t):
+    if t["link"] == "core" or t["link"] is None:
+        return RATE["core"]
+    return RATE["o"] if t["key"][0][0] == "o" else RATE[t["link"][0]]
+
+
 def schedule():
     left = transfers() + computes()
     for t in left:
-        rate = 200e3 if t["link"] == "core" else 45e3
+        rate = rate_of(t)
         if t["link"] is not None:
             t["time"] = t["size"] / rate
     done, free, order, now = {}, {}, [], 0.0
@@ -201,7 +210,7 @@
         else:
             now += 0.1
             free[t["link"]] = max(now, free.get(t["link"], 0.0)) + t["time"]
-            done[t["key"]] = free[t["link"]] + 1.5
+            done[t["key"]] = free[t["link"]] + LATENCY
         order.append(t)
         left.remove(t)
     return order, done
@@ -322,14 +331,14 @@
             mine = other == 0 and (what == "ring" or what == "pair" and step == 0)
             return copy(source() if mine else block(slot[0]), block(slot[0]), to)
         lo, hi = COLS[kind[1]][ch]
-        whole, count = (w1, W1) if kind[0] == "v" else (w2, W2)
+        whole, count, skip = (w1, W1, 0) if kind[0] == "v" else (w2, W2, 16)
         if what == "x":
             slot, to = at(dz=-step), at(dxl=1)
         elif what == "ring":
             slot, to = at(dxl=other), at(dz=step)
         else:
             slot, to = at(dxl=other, dz=-step), at(dz=step)
-        dst = whole.at[pl.ds(slot[1] * count, count), pl.ds(lo, hi - lo)]
+        dst = whole.at[pl.ds(slot[1] * count + skip, count - skip), pl.ds(lo, hi - lo)]
         return copy(dst, dst, to)
 
     def merge(part, ch):
@@ -418,6 +427,10 @@
                     qkv_s[s, k, pl.ds((m * 4 + j) * SHARD, SHARD), :] = result[
                         j * W1 + k * SHARD : j * W1 + (k + 1) * SHARD
                     ]
+
+    def fill():
+        for c in range(8):
+            w2[pl.ds(c * W2, 16), :] = w1[pl.ds(c * W1 + W2_FROM, 16), :]
 
     def head(first, second, keys, s, rows):
         cosine, sine = cos_ref[...], sin_ref[...]
@@ -479,7 +492,7 @@
         for dep in t["sends"]:
             copies[dep].wait_send()
             gone.add(dep)
-        dict(merge=merge, columns=columns, stat=stat, moments=get_moments, norm=norm, qkv=qkv, attend=attend, out=project)[key[0]](*key[1:])
+        dict(merge=merge, columns=columns, stat=stat, moments=get_moments, norm=norm, qkv=qkv, fill=fill, attend=attend, out=project)[key[0]](*key[1:])
     for key in sorted(copies, key=lambda k: done[k]):
         if key not in waited:
             copies[key].wait_recv()

time: 152 us -> 143 us (0.941)
  Pallas kernels: 150 us -> 141 us
    pallas_call x1, Pallas kernels: 150 us -> 141 us  [run_fused(): pl.pallas_call(fused, out_shape=jax.ShapeDtypeStruct((PART, TOK), jnp.bfl...]
where the time goes in v5:
time: 143 us
  Pallas kernels  141 us (99%)
  local copies, waits for them, and re-layouts  1.97 us (1%)
    pallas_call x1, Pallas kernels, run_fused(): pl.pallas_call(fused, out_shape=jax.ShapeDtypeStruct((PART, TOK), jnp.bfl...  141 us

profile of v5, /device:TPU:1, one launch (start us, length us, event | category | flops | bytes accessed | tf_op | source)
XLA Modules:
  0.0 143.2 jit_solution(13717407139186917676)
XLA Ops:
  0.0 141.2 %shard_map.91 = bf16[320,1024]{1,0:T(8,128)(2,1)} custom-call(bf16[320,8192]{1,0:T(8,128)(2,1)} %bitcast.8, f32[160,5120]{1,0:T(8,128)} %bitcast.10, f32[256,5120]{1,0:T(8,128)} %bitcast.9, s32[1,32]{1,0:T(1,128)} %bitcast.15, f32[160,64]{1,0:T(8,128)} %bitcast.12, f32[40,128]{1,0:T(8,128)} %bitcast.13, f32[40,128]{1,0:T(8,128)} %bitcast.14, ...), custom_call_target="tpu_custom_call" | custom-call | tf_op jit(solution)/shard_map/pallas_call | solution.py:514
  141.2 2.0 %copy.11 = bf16[1024,320]{0,1:T(8,128)(2,1)} copy(bf16[1024,320]{0,1:T(8,128)(2,1)} %bitcast.11) | data formatting | bytes 1310720

commit v6 on v5

--- a/solution.py
+++ b/solution.py
@@ -30,6 +30,7 @@
 COLS = {"p": [(0, 768), (768, 1792)], "s": [(1792, 3584), (3584, D)]}
 LATE = (3,)
 SLACK = 3.0
+UNROLL = 4
 RATE = {"core": 100e3, "o": 30e3, "y": 40e3, "z": 42e3, "x": 40e3, "c": 40e3}
 LATENCY = 2.5
 
@@ -393,7 +394,7 @@
             x = t1[pl.ds(pl.multiple_of(base + i * 16, 16), 16), :].astype(jnp.float32) * mask_ref[...]
             return one + x[:8] + x[8:], two + x[:8] * x[:8] + x[8:] * x[8:]
 
-        one, two = lax.fori_loop(0, PART // 16, body, (sums[0], sums[1]))
+        one, two = lax.fori_loop(0, PART // 16, body, (sums[0], sums[1]), unroll=UNROLL)
         sums[0] = one
         sums[1] = two
 
@@ -414,7 +415,7 @@
             t1[here, :] = ((x - moments[0]) * moments[1] * gain + shift).astype(jnp.bfloat16)
             return carry
 
-        lax.fori_loop(0, PART // 16, body, 0)
+        lax.fori_loop(0, PART // 16, body, 0, unroll=UNROLL)
 
     def qkv(s):
         lanes = pl.ds(pl.multiple_of(protein(core, s) * LEN, LEN), LEN)

time: 143 us -> 138 us (0.965)
  Pallas kernels: 141 us -> 136 us
    pallas_call x1, Pallas kernels: 141 us -> 136 us  [run_fused(): pl.pallas_call(fused, out_shape=jax.ShapeDtypeStruct((PART, TOK), jnp.bfl...]
where the time goes in v6:
time: 138 us
  Pallas kernels  136 us (99%)
  local copies, waits for them, and re-layouts  1.97 us (1%)
    pallas_call x1, Pallas kernels, run_fused(): pl.pallas_call(fused, out_shape=jax.ShapeDtypeStruct((PART, TOK), jnp.bfl...  136 us

profile of v6, /device:TPU:1, one launch (start us, length us, event | category | flops | bytes accessed | tf_op | source)
XLA Modules:
  0.0 138.3 jit_solution(14775371309941231970)
XLA Ops:
  0.0 136.3 %shard_map.91 = bf16[320,1024]{1,0:T(8,128)(2,1)} custom-call(bf16[320,8192]{1,0:T(8,128)(2,1)} %bitcast.8, f32[160,5120]{1,0:T(8,128)} %bitcast.10, f32[256,5120]{1,0:T(8,128)} %bitcast.9, s32[1,32]{1,0:T(1,128)} %bitcast.15, f32[160,64]{1,0:T(8,128)} %bitcast.12, f32[40,128]{1,0:T(8,128)} %bitcast.13, f32[40,128]{1,0:T(8,128)} %bitcast.14, ...), custom_call_target="tpu_custom_call" | custom-call | tf_op jit(solution)/shard_map/pallas_call | solution.py:515
  136.3 2.0 %copy.11 = bf16[1024,320]{0,1:T(8,128)(2,1)} copy(bf16[1024,320]{0,1:T(8,128)(2,1)} %bitcast.11) | data formatting | bytes 1310720

commit v7 on v6

--- a/solution.py
+++ b/solution.py
@@ -28,7 +28,7 @@
 
 
 COLS = {"p": [(0, 768), (768, 1792)], "s": [(1792, 3584), (3584, D)]}
-LATE = (3,)
+LATE = (2,)
 SLACK = 3.0
 UNROLL = 4
 RATE = {"core": 100e3, "o": 30e3, "y": 40e3, "z": 42e3, "x": 40e3, "c": 40e3}

time: 138 us -> 137 us (level)
  no operation moved by 1% of the time
where the time goes in v7:
time: 137 us
  Pallas kernels  135 us (99%)
  local copies, waits for them, and re-layouts  1.97 us (1%)
    pallas_call x1, Pallas kernels, run_fused(): pl.pallas_call(fused, out_shape=jax.ShapeDtypeStruct((PART, TOK), jnp.bfl...  135 us

profile of v7, /device:TPU:1, one launch (start us, length us, event | category | flops | bytes accessed | tf_op | source)
XLA Modules:
  0.0 136.9 jit_solution(12761224446953922736)
XLA Ops:
  0.0 134.9 %shard_map.91 = bf16[320,1024]{1,0:T(8,128)(2,1)} custom-call(bf16[320,8192]{1,0:T(8,128)(2,1)} %bitcast.8, f32[160,5120]{1,0:T(8,128)} %bitcast.10, f32[256,5120]{1,0:T(8,128)} %bitcast.9, s32[1,32]{1,0:T(1,128)} %bitcast.15, f32[160,64]{1,0:T(8,128)} %bitcast.12, f32[40,128]{1,0:T(8,128)} %bitcast.13, f32[40,128]{1,0:T(8,128)} %bitcast.14, ...), custom_call_target="tpu_custom_call" | custom-call | tf_op jit(solution)/shard_map/pallas_call | solution.py:515
  135.0 2.0 %copy.11 = bf16[1024,320]{0,1:T(8,128)(2,1)} copy(bf16[1024,320]{0,1:T(8,128)(2,1)} %bitcast.11) | data formatting | bytes 1310720
